TPU v7x, 256 devices: a whole 4x4x8 slice. The times are simulated.
256 devices in a mesh: seq: 32 (over x, z), mp: 8 (over y, core).
Axes of the slice: x: 4, y: 4, z: 8, core: 2. Of those that a mesh axis runs over, the one named last changes fastest.
Arguments:
- queries: bfloat16 [16384, 3072], P(('seq', 'mp')), may hold values from -128 to 128
- keys: bfloat16 [16384, 3072], P(('seq', 'mp')), may hold values from -4 to 4
- values: bfloat16 [16384, 3072], P(('seq', 'mp')), may hold values from -6 to 6
- out_grad: bfloat16 [16384, 3072], P(('seq', 'mp')), may hold values from -6 to 6
- window_lists: int32 [256, 27], P('seq'), may hold values from -1 to 255, as said below
- valid_counts: int32 [256], replicated, may hold values from 1 to 64, as said below
Outputs:
- attended: bfloat16 [16384, 3072], P(('seq', 'mp'))
- grad_queries: bfloat16 [16384, 3072], P(('seq', 'mp'))
- grad_keys: bfloat16 [16384, 3072], P(('seq', 'mp'))
- grad_values: bfloat16 [16384, 3072], P(('seq', 'mp'))
Inputs may be any that keep to these rules, and one draw needn't show every extreme that they name: `window_lists`: each tile's list holds the tile itself and some of the other tiles of its 3 x 3 x 3 block of tiles inside the grid of 8 x 8 x 4 tiles, each at most once, and -1 in the other slots. `valid_counts`: tiles that are not in the last tile layer or the last tile row hold 64 valid tokens.
All inputs are finite; a program needn't handle non-finite values.
Results may differ from a plain program's by a relative error of at most 0.006.
Values may be sent and summed in bfloat16 or wider, within the bound.
A program may use at most 128 MiB of HBM per device.

v0:
```python
import math

import jax
import jax.numpy as jnp
from jax import lax
from jax.sharding import PartitionSpec as P

HEAD_DIM = 128
TILE = 64
WINDOW = 27
TLAYERS = 8
TH_DEV = 2
TW = 4


def from_behind(value, axis, by):
    count = lax.axis_size(axis)
    pairs = [(i, i + by) for i in range(count) if 0 <= i + by < count]
    return lax.ppermute(value, axis, pairs)


def window_direct(center, layer_devs):
    depth = center.shape[0]
    pool = jnp.zeros((3, depth + 2) + center.shape[1:], center.dtype)
    pool = pool.at[1, 1 : depth + 1].set(center)
    for step_t in (-1, 0, 1):
        for step_h in (-1, 0, 1):
            needed = not (step_t == 0 and step_h == 0) and (not (layer_devs == 1 and step_h != 0))
            if needed:
                came = from_behind(center, "seq", -(step_t * layer_devs + step_h))
                if step_h < 0:
                    pool = pool.at[step_t + 1, 0].set(came[depth - 1])
                elif step_h == 0:
                    pool = pool.at[step_t + 1, 1 : depth + 1].set(came)
                else:
                    pool = pool.at[step_t + 1, depth + 1].set(came[0])
    return pool


def return_direct(grad_pool, layer_devs):
    depth = grad_pool.shape[1] - 2
    own = grad_pool[1, 1 : depth + 1]
    for step_t in (-1, 0, 1):
        for step_h in (-1, 0, 1):
            needed = not (step_t == 0 and step_h == 0) and (not (layer_devs == 1 and step_h != 0))
            if needed:
                if step_h < 0:
                    region = grad_pool[step_t + 1, 0:1]
                elif step_h == 0:
                    region = grad_pool[step_t + 1, 1 : depth + 1]
                else:
                    region = grad_pool[step_t + 1, depth + 1 : depth + 2]
                back = from_behind(region, "seq", step_t * layer_devs + step_h)
                if step_h < 0:
                    own = own.at[depth - 1 : depth].add(back)
                elif step_h == 0:
                    own = own + back
                else:
                    own = own.at[0:1].add(back)
    return own


def attend_block(key_pool, value_pool, block):
    query_b, cot_b, slot_b, key_ok, query_ok = block
    heads, count = (query_b.shape[0], query_b.shape[1])
    scale = 1.0 / math.sqrt(HEAD_DIM)
    flat_slots = slot_b.reshape(-1)
    key_win = key_pool[:, flat_slots].reshape(heads, count, WINDOW * TILE, HEAD_DIM)
    value_win = value_pool[:, flat_slots].reshape(heads, count, WINDOW * TILE, HEAD_DIM)
    scores = (
        jnp.einsum("hcqd,hckd->hcqk", query_b, key_win, preferred_element_type=jnp.float32) * scale
    )
    scores = jnp.where(key_ok[None, :, None, :], scores, -1e30)
    top = jnp.max(scores, axis=-1, keepdims=True)
    expo = jnp.exp(scores - top)
    probs = expo / jnp.sum(expo, axis=-1, keepdims=True)
    probs_low = probs.astype(jnp.bfloat16)
    attended = jnp.einsum(
        "hcqk,hckd->hcqd", probs_low, value_win, preferred_element_type=jnp.float32
    )
    attended = (attended * query_ok.astype(jnp.float32)[None, :, :, None]).astype(jnp.bfloat16)
    delta = jnp.sum(cot_b.astype(jnp.float32) * attended.astype(jnp.float32), axis=-1)
    dprobs = jnp.einsum("hcqd,hckd->hcqk", cot_b, value_win, preferred_element_type=jnp.float32)
    dscores = (probs * (dprobs - delta[:, :, :, None]) * scale).astype(jnp.bfloat16)
    grad_q = jnp.einsum(
        "hcqk,hckd->hcqd", dscores, key_win, preferred_element_type=jnp.float32
    ).astype(jnp.bfloat16)
    grad_k = jnp.einsum("hcqk,hcqd->hckd", dscores, query_b, preferred_element_type=jnp.float32)
    grad_v = jnp.einsum("hcqk,hcqd->hckd", probs_low, cot_b, preferred_element_type=jnp.float32)
    grad_k = grad_k.reshape(heads, count * WINDOW, TILE, HEAD_DIM)
    grad_v = grad_v.reshape(heads, count * WINDOW, TILE, HEAD_DIM)
    return (attended, grad_q, grad_k, grad_v)


def on_device(queries, keys, values, out_grad, window_lists, valid_counts):
    query_t, key_t, value_t, cot_t = (
        lax.all_to_all(queries, "mp", split_axis=1, concat_axis=0, tiled=True),
        lax.all_to_all(keys, "mp", split_axis=1, concat_axis=0, tiled=True),
        lax.all_to_all(values, "mp", split_axis=1, concat_axis=0, tiled=True),
        lax.all_to_all(out_grad, "mp", split_axis=1, concat_axis=0, tiled=True),
    )
    rows, width = query_t.shape
    heads = width // HEAD_DIM
    tiles_dev = rows // TILE
    layer_devs = lax.axis_size("seq") // TLAYERS
    grid_rows = layer_devs * TH_DEV
    seat = lax.axis_index("seq")
    center = jnp.concatenate([key_t, value_t], axis=1).reshape(TH_DEV, TW * TILE, 2 * width)
    pool = window_direct(center, layer_devs)
    pool_count = 3 * (TH_DEV + 2) * TW
    pool_split = pool.reshape(pool_count, TILE, 2, heads, HEAD_DIM)
    key_pool = jnp.transpose(pool_split[:, :, 0], (2, 0, 1, 3))
    value_pool = jnp.transpose(pool_split[:, :, 1], (2, 0, 1, 3))
    live = window_lists >= 0
    safe = jnp.maximum(window_lists, 0)
    layer = safe // (grid_rows * TW)
    grid_row = safe // TW % grid_rows
    column = safe % TW
    layer_first = seat // layer_devs
    row_first = seat % layer_devs * TH_DEV
    slots = ((layer - layer_first + 1) * (TH_DEV + 2) + (grid_row - row_first + 1)) * TW + column
    slots = jnp.where(live, slots, 0)
    total_tiles = valid_counts.shape[0]
    matches = safe.reshape(-1)[:, None] == jnp.arange(total_tiles, dtype=jnp.int32)[None, :]
    key_count = jnp.sum(jnp.where(matches, valid_counts[None, :], 0), axis=1).reshape(
        tiles_dev, WINDOW
    )
    places = jnp.arange(TILE, dtype=jnp.int32)
    key_ok = (live[:, :, None] & (places[None, None, :] < key_count[:, :, None])).reshape(
        tiles_dev, WINDOW * TILE
    )
    own_count = lax.dynamic_slice_in_dim(valid_counts, seat * tiles_dev, tiles_dev)
    query_ok = places[None, :] < own_count[:, None]
    half = tiles_dev // 2
    cot_masked = cot_t.reshape(tiles_dev, TILE, width) * query_ok[:, :, None].astype(jnp.bfloat16)

    def head_major(array):
        return jnp.transpose(array.reshape(2, half, TILE, heads, HEAD_DIM), (0, 3, 1, 2, 4))

    def split(array):
        return array.reshape((2, half) + array.shape[1:])

    blocks = (
        head_major(query_t),
        head_major(cot_masked),
        split(slots),
        split(key_ok),
        split(query_ok),
    )

    def one_block(carry, block):
        grad_kp, grad_vp = carry
        attended, grad_q, grad_k, grad_v = attend_block(key_pool, value_pool, block)
        where_to = block[2].reshape(-1)
        grad_kp = grad_kp.at[:, where_to].add(grad_k)
        grad_vp = grad_vp.at[:, where_to].add(grad_v)
        return ((grad_kp, grad_vp), (attended, grad_q))

    start = jnp.zeros((heads, pool_count, TILE, HEAD_DIM), jnp.float32)
    (grad_kp, grad_vp), outputs = lax.scan(one_block, (start, start), blocks)

    def token_major(array):
        return jnp.transpose(array, (0, 2, 3, 1, 4)).reshape(rows, width)

    attended = token_major(outputs[0])
    grad_q = token_major(outputs[1])

    def pool_major(array):
        return jnp.transpose(array, (1, 2, 0, 3)).reshape(3, TH_DEV + 2, TW * TILE, width)

    grad_pool = jnp.concatenate([pool_major(grad_kp), pool_major(grad_vp)], axis=-1)
    own = return_direct(grad_pool, layer_devs)
    own = own.reshape(rows, 2 * width)
    grad_k = own[:, :width].astype(jnp.bfloat16)
    grad_v = own[:, width:].astype(jnp.bfloat16)
    return (
        lax.all_to_all(attended, "mp", split_axis=0, concat_axis=1, tiled=True),
        lax.all_to_all(grad_q, "mp", split_axis=0, concat_axis=1, tiled=True),
        lax.all_to_all(grad_k, "mp", split_axis=0, concat_axis=1, tiled=True),
        lax.all_to_all(grad_v, "mp", split_axis=0, concat_axis=1, tiled=True),
    )


def solution(mesh):
    in_specs = (
        P(("seq", "mp"), None),
        P(("seq", "mp"), None),
        P(("seq", "mp"), None),
        P(("seq", "mp"), None),
        P("seq", None),
        P(),
    )
    out_specs = (
        P(("seq", "mp"), None),
        P(("seq", "mp"), None),
        P(("seq", "mp"), None),
        P(("seq", "mp"), None),
    )
    return jax.shard_map(
        on_device, mesh=mesh, in_specs=in_specs, out_specs=out_specs, check_vma=False
    )
```

profile of v0, /device:TPU:68, one launch (start us, length us, event | category | flops | bytes accessed | tf_op | source)
XLA Modules:
  0.0 906.9 jit_solution(3455932290881480363)
XLA Ops:
  2.4 4.5 all-to-all-start.1
  18.7 4.8 all-to-all-start.2
  23.5 8.9 all-to-all-done.2
  32.4 3.5 all-to-all-start.3
  36.6 6.8 collective-permute-start.7
  43.4 2.9 collective-permute-start.3
  48.3 8.3 collective-permute-start.1
  56.6 2.8 collective-permute-start
  59.4 4.7 all-to-all-start
  64.1 3.0 fusion.45
  68.0 5.1 all-to-all-done
  74.1 69.1 %collective-permute-done = bf16[2,256,768]{2,1,0:T(8,128)(2,1)} collective-permute-done((bf16[2,256,768]{2,1,0:T(8,128)(2,1)S(1)}, bf16[2,256,768]{2,1,0:T(8,128)(2,1)}, u32[]{:S(2)}, u32[]{:S(2)}) %collective-permute-start) | collective-permute-done | bytes 786464 | tf_op jit(solution)/shard_map/ppermute | solution.py:19
  147.6 49.6 %collective-permute-done.1 = bf16[2,256,768]{2,1,0:T(8,128)(2,1)S(1)} collective-permute-done((bf16[2,256,768]{2,1,0:T(8,128)(2,1)S(1)}, bf16[2,256,768]{2,1,0:T(8,128)(2,1)S(1)}, u32[]{:S(2)}, u32[]{:S(2)}) %collective-permute-start.1) | collective-permute-done | bytes 786464 | tf_op jit(solution)/shard_map/ppermute | solution.py:19
  201.2 17.6 %collective-permute-done.2 = bf16[2,256,768]{2,1,0:T(8,128)(2,1)} collective-permute-done((bf16[2,256,768]{2,1,0:T(8,128)(2,1)S(1)}, bf16[2,256,768]{2,1,0:T(8,128)(2,1)}, u32[]{:S(2)}, u32[]{:S(2)}) %collective-permute-start.2) | collective-permute-done | bytes 786464 | tf_op jit(solution)/shard_map/ppermute | solution.py:19
  220.7 4.0 fusion.59
  227.3 40.3 %collective-permute-done.5 = bf16[2,256,768]{2,1,0:T(8,128)(2,1)S(1)} collective-permute-done((bf16[2,256,768]{2,1,0:T(8,128)(2,1)S(1)}, bf16[2,256,768]{2,1,0:T(8,128)(2,1)S(1)}, u32[]{:S(2)}, u32[]{:S(2)}) %collective-permute-start.5) | collective-permute-done | bytes 786464 | tf_op jit(solution)/shard_map/ppermute | solution.py:19
  271.1 11.3 %reshape.721 = bf16[48,64,2,3,128]{4,3,2,1,0:T(4,128)(2,1)} reshape(bf16[3,4,256,768]{3,2,1,0:T(8,128)(2,1)} %fusion.54) | data formatting | bytes 9437184 | tf_op jit(solution)/shard_map/reshape | solution.py:111
  282.4 4.8 slice_bitcast_fusion
  289.9 2.7 broadcast_in_dim.36.clone
  295.3 240.5 %while.31 = (s32[]{:T(128)}, f32[3,48,64,128]{3,2,1,0:T(8,128)}, f32[3,48,64,128]{3,2,1,0:T(8,128)}, bf16[2,3,4,64,128]{4,3,2,1,0:T(8,128)(2,1)}, bf16[2,3,4,64,...) while((s32[]{:T(128)}, f32[3,48,64,128]{3,2,1,0:T(8,128)}, ...), condition=%wide.region_8.0_spmd, body=%wide.region_2.8_spmd.sunk | while | flops 2061683200 | bytes 291334816 | solution.py:160
  295.9 5.3 gather_fusion.1
  301.2 6.6 copy.111
  307.8 3.7 gather_fusion
  311.4 6.4 copy.110
  317.9 7.1 fusion.114
  325.0 5.5 multiply_reduce_fusion.2
  337.0 4.1 fusion.116
  341.1 5.2 copy.113
  346.3 28.4 %scatter_fusion.1 = f32[3,48,64,128]{3,2,1,0:T(8,128)} fusion(f32[3,48,64,128]{3,2,1,0:T(8,128)} %get-tuple-element.447, s32[108]{0:T(128)S(1)} %fusion.113, f32[108,3,64,128]{3,2,1,0:T(8,128)} %bitcast.216), kind=kCustom, calls=%fused_computation.3.clone.1 | custom fusion | flops 2654208 | bytes 31850928 | tf_op jit(solution)/shard_map/while/body/eval_jaxpr/scatter-add | solution.py:156
  374.7 3.5 fusion.115
  378.1 5.2 copy.112
  383.3 28.5 %scatter_fusion = f32[3,48,64,128]{3,2,1,0:T(8,128)} fusion(f32[3,48,64,128]{3,2,1,0:T(8,128)} %get-tuple-element.446, s32[108]{0:T(128)S(1)} %fusion.113, f32[108,3,64,128]{3,2,1,0:T(8,128)} %bitcast.215), kind=kCustom, calls=%fused_computation.2.clone.1 | custom fusion | flops 2654208 | bytes 31850928 | tf_op jit(solution)/shard_map/while/body/eval_jaxpr/scatter-add | solution.py:155
  412.0 5.3 gather_fusion.1
  417.3 6.6 copy.111
  423.9 3.7 gather_fusion
  427.5 6.4 copy.110
  434.0 7.1 fusion.114
  441.1 5.5 multiply_reduce_fusion.2
  453.1 4.1 fusion.116
  457.2 5.2 copy.113
  462.4 28.4 %scatter_fusion.1 = f32[3,48,64,128]{3,2,1,0:T(8,128)} fusion(f32[3,48,64,128]{3,2,1,0:T(8,128)} %get-tuple-element.447, s32[108]{0:T(128)S(1)} %fusion.113, f32[108,3,64,128]{3,2,1,0:T(8,128)} %bitcast.216), kind=kCustom, calls=%fused_computation.3.clone.1 | custom fusion | flops 2654208 | bytes 31850928 | tf_op jit(solution)/shard_map/while/body/eval_jaxpr/scatter-add | solution.py:156
  490.8 3.5 fusion.115
  494.3 5.2 copy.112
  499.5 28.4 %scatter_fusion = f32[3,48,64,128]{3,2,1,0:T(8,128)} fusion(f32[3,48,64,128]{3,2,1,0:T(8,128)} %get-tuple-element.446, s32[108]{0:T(128)S(1)} %fusion.113, f32[108,3,64,128]{3,2,1,0:T(8,128)} %bitcast.215), kind=kCustom, calls=%fused_computation.2.clone.1 | custom fusion | flops 2654208 | bytes 31850928 | tf_op jit(solution)/shard_map/while/body/eval_jaxpr/scatter-add | solution.py:155
  535.9 9.2 %copy.82 = f32[48,64,3,128]{3,2,1,0:T(4,128)} copy(f32[48,64,3,128]{3,1,0,2:T(8,128)} %bitcast.219) | data formatting | bytes 9437184 | tf_op jit(solution)/shard_map/transpose | solution.py:169
  545.1 8.5 reshape.723
  553.6 5.0 constant_dynamic-update-slice_fusion.1
  558.7 6.9 copy.83
  565.5 8.5 reshape.724
  574.1 5.0 constant_dynamic-update-slice_fusion
  579.1 4.6 slice_bitcast_fusion.2
  583.7 4.6 collective-permute-start.9
  590.3 17.3 %collective-permute-start.8 = (f32[1,256,768]{2,1,0:T(8,128)}, f32[1,256,768]{2,1,0:T(8,128)}, u32[]{:S(2)}, u32[]{:S(2)}) collective-permute-start(f32[1,256,768]{2,1,0:T(8,128)} %get-tuple-element.336), channel_id=1, source_target_pairs={{40,0},{48,8},{56,16},{64,24},{72,32},{80,40},{88,48},{96,56},{104... | collective-permute-start | bytes 2359304 | tf_op jit(solution)/shard_map/ppermute | solution.py:19
  607.7 12.0 %collective-permute-start.10 = (f32[1,256,768]{2,1,0:T(8,128)}, f32[1,256,768]{2,1,0:T(8,128)}, u32[]{:S(2)}, u32[]{:S(2)}) collective-permute-start(f32[1,256,768]{2,1,0:T(8,128)} %get-tuple-element.335), channel_id=1, source_target_pairs={{24,0},{32,8},{40,16},{48,24},{56,32},{64,40},{72,48},{80,56},{88,... | collective-permute-start | bytes 2359304 | tf_op jit(solution)/shard_map/ppermute | solution.py:19
  625.2 7.6 all-to-all-start.5
  635.2 74.6 %collective-permute-done.8 = f32[1,256,768]{2,1,0:T(8,128)} collective-permute-done((f32[1,256,768]{2,1,0:T(8,128)}, f32[1,256,768]{2,1,0:T(8,128)}, u32[]{:S(2)}, u32[]{:S(2)}) %collective-permute-start.8) | collective-permute-done | bytes 786464 | tf_op jit(solution)/shard_map/ppermute | solution.py:19
  716.7 38.2 %collective-permute-start.13 = (f32[1,256,768]{2,1,0:T(8,128)S(1)}, f32[1,256,768]{2,1,0:T(8,128)S(1)}, u32[]{:S(2)}, u32[]{:S(2)}) collective-permute-start(f32[1,256,768]{2,1,0:T(8,128)S(1)} %copy-done.4), channel_id=1, source_target_pairs={{0,24},{8,32},{16,40},{24,48},{32,56},{40,64},{48,72},{56,80},{64,... | collective-permute-start | bytes 2359304 | tf_op jit(solution)/shard_map/ppermute | solution.py:19
  756.2 28.6 %collective-permute-done.11 = f32[1,256,768]{2,1,0:T(8,128)} collective-permute-done((f32[1,256,768]{2,1,0:T(8,128)}, f32[1,256,768]{2,1,0:T(8,128)}, u32[]{:S(2)}, u32[]{:S(2)}) %collective-permute-start.11) | collective-permute-done | bytes 786464 | tf_op jit(solution)/shard_map/ppermute | solution.py:19
  786.3 27.4 %collective-permute-done.13 = f32[1,256,768]{2,1,0:T(8,128)S(1)} collective-permute-done((f32[1,256,768]{2,1,0:T(8,128)S(1)}, f32[1,256,768]{2,1,0:T(8,128)S(1)}, u32[]{:S(2)}, u32[]{:S(2)}) %collective-permute-start.13) | collective-permute-done | bytes 786464 | tf_op jit(solution)/shard_map/ppermute | solution.py:19
  815.5 17.7 %all-to-all-start.4 = ((bf16[8,64,384]{2,1,0:T(8,128)(2,1)}), bf16[8,64,384]{2,1,0:T(8,128)(2,1)S(1)}, u32[]{:S(2)}, u32[]{:S(2)}) async-start(bf16[8,64,384]{2,1,0:T(8,128)(2,1)} %all_to_all.116), calls=%async_computation.4 | async-start | bytes 786432 | tf_op jit(solution)/shard_map/all_to_all | solution.py:177
  833.2 40.1 %collective-permute-done.15 = f32[1,256,768]{2,1,0:T(8,128)} collective-permute-done((f32[1,256,768]{2,1,0:T(8,128)S(1)}, f32[1,256,768]{2,1,0:T(8,128)}, u32[]{:S(2)}, u32[]{:S(2)}) %collective-permute-start.15) | collective-permute-done | bytes 786464 | tf_op jit(solution)/shard_map/ppermute | solution.py:19
  875.5 18.0 %all_to_all.140 = bf16[8,64,384]{2,1,0:T(8,128)(2,1)S(1)} all-to-all(bf16[8,64,384]{2,1,0:T(8,128)(2,1)S(1)} %bitcast.241), channel_id=1, replica_groups=mesh['seq'=32,'mp'=8] {'mp'}, dimensions={0} | all-to-all | bytes 786432 | tf_op jit(solution)/shard_map/all_to_all | solution.py:179
  893.5 3.5 all-to-all-start.7
  899.4 6.5 all-to-all-done.7
  (134 shorter events, 79.6 us)
Async XLA Ops:
  2.4 16.3 %all-to-all-start.1 = ((bf16[64,8,384]{2,0,1:T(8,128)(2,1)}), bf16[64,8,384]{2,0,1:T(8,128)(2,1)S(1)}, u32[]{:S(2)}, u32[]{:S(2)}) async-start(bf16[64,8,384]{2,0,1:T(8,128)(2,1)} %bitcast.165), calls=%async_computation.1 | async-start | bytes 786432 | tf_op jit(solution)/shard_map/all_to_all | solution.py:98
  18.7 13.7 %all-to-all-start.2 = ((bf16[64,8,384]{2,0,1:T(8,128)(2,1)}), bf16[64,8,384]{2,0,1:T(8,128)(2,1)S(1)}, u32[]{:S(2)}, u32[]{:S(2)}) async-start(bf16[64,8,384]{2,0,1:T(8,128)(2,1)} %bitcast.164), calls=%async_computation.2 | async-start | bytes 786432 | tf_op jit(solution)/shard_map/all_to_all | solution.py:99
  32.4 27.0 %all-to-all-start.3 = ((bf16[64,8,384]{2,0,1:T(8,128)(2,1)}), bf16[64,8,384]{2,0,1:T(8,128)(2,1)S(1)}, u32[]{:S(2)}, u32[]{:S(2)}) async-start(bf16[64,8,384]{2,0,1:T(8,128)(2,1)} %bitcast.163), calls=%async_computation.3 | async-start | bytes 786432 | tf_op jit(solution)/shard_map/all_to_all | solution.py:100
  36.6 232.7 %collective-permute-start.7 = (bf16[2,256,768]{2,1,0:T(8,128)(2,1)S(1)}, bf16[2,256,768]{2,1,0:T(8,128)(2,1)}, u32[]{:S(2)}, u32[]{:S(2)}) collective-permute-start(bf16[2,256,768]{2,1,0:T(8,128)(2,1)S(1)} %pad_maximum_fusion), channel_id=1, source_target_pairs={{40,0},{48,8},{56,16},{64,24},{72,32},{80,40},{88,48},{96,56},{104... | collective-permute-start | bytes 2359304 | tf_op jit(solution)/shard_map/ppermute | solution.py:19
  43.4 181.3 %collective-permute-start.3 = (bf16[2,256,768]{2,1,0:T(8,128)(2,1)S(1)}, bf16[2,256,768]{2,1,0:T(8,128)(2,1)}, u32[]{:S(2)}, u32[]{:S(2)}) collective-permute-start(bf16[2,256,768]{2,1,0:T(8,128)(2,1)S(1)} %pad_maximum_fusion), channel_id=1, source_target_pairs={{0,8},{8,16},{16,24},{24,32},{32,40},{40,48},{48,56},{56,64},{64,7... | collective-permute-start | bytes 2359304 | tf_op jit(solution)/shard_map/ppermute | solution.py:19
  46.3 172.5 %collective-permute-start.2 = (bf16[2,256,768]{2,1,0:T(8,128)(2,1)S(1)}, bf16[2,256,768]{2,1,0:T(8,128)(2,1)}, u32[]{:S(2)}, u32[]{:S(2)}) collective-permute-start(bf16[2,256,768]{2,1,0:T(8,128)(2,1)S(1)} %pad_maximum_fusion), channel_id=1, source_target_pairs={{0,24},{8,32},{16,40},{24,48},{32,56},{40,64},{48,72},{56,80},{64,... | collective-permute-start | bytes 2359304 | tf_op jit(solution)/shard_map/ppermute | solution.py:19
  48.3 148.9 %collective-permute-start.1 = (bf16[2,256,768]{2,1,0:T(8,128)(2,1)S(1)}, bf16[2,256,768]{2,1,0:T(8,128)(2,1)S(1)}, u32[]{:S(2)}, u32[]{:S(2)}) collective-permute-start(bf16[2,256,768]{2,1,0:T(8,128)(2,1)S(1)} %pad_maximum_fusion), channel_id=1, source_target_pairs={{0,32},{8,40},{16,48},{24,56},{32,64},{40,72},{48,80},{56,88},{64,... | collective-permute-start | bytes 2359304 | tf_op jit(solution)/shard_map/ppermute | solution.py:19
  56.6 86.7 %collective-permute-start = (bf16[2,256,768]{2,1,0:T(8,128)(2,1)S(1)}, bf16[2,256,768]{2,1,0:T(8,128)(2,1)}, u32[]{:S(2)}, u32[]{:S(2)}) collective-permute-start(bf16[2,256,768]{2,1,0:T(8,128)(2,1)S(1)} %pad_maximum_fusion), channel_id=1, source_target_pairs={{0,40},{8,48},{16,56},{24,64},{32,72},{40,80},{48,88},{56,96},{64,... | collective-permute-start | bytes 2359304 | tf_op jit(solution)/shard_map/ppermute | solution.py:19
  59.4 13.7 %all-to-all-start = ((bf16[64,8,384]{2,0,1:T(8,128)(2,1)}), bf16[64,8,384]{2,0,1:T(8,128)(2,1)S(1)}, u32[]{:S(2)}, u32[]{:S(2)}) async-start(bf16[64,8,384]{2,0,1:T(8,128)(2,1)} %bitcast.166), calls=%async_computation | async-start | bytes 786432 | tf_op jit(solution)/shard_map/all_to_all | solution.py:97
  143.3 83.2 %collective-permute-start.4 = (bf16[2,256,768]{2,1,0:T(8,128)(2,1)S(1)}, bf16[2,256,768]{2,1,0:T(8,128)(2,1)S(1)}, u32[]{:S(2)}, u32[]{:S(2)}) collective-permute-start(bf16[2,256,768]{2,1,0:T(8,128)(2,1)S(1)} %pad_maximum_fusion), channel_id=1, source_target_pairs={{8,0},{16,8},{24,16},{32,24},{40,32},{48,40},{56,48},{64,56},{72,6... | collective-permute-start | bytes 2359304 | tf_op jit(solution)/shard_map/ppermute | solution.py:19
  197.2 70.4 %collective-permute-start.5 = (bf16[2,256,768]{2,1,0:T(8,128)(2,1)S(1)}, bf16[2,256,768]{2,1,0:T(8,128)(2,1)S(1)}, u32[]{:S(2)}, u32[]{:S(2)}) collective-permute-start(bf16[2,256,768]{2,1,0:T(8,128)(2,1)S(1)} %pad_maximum_fusion), channel_id=1, source_target_pairs={{24,0},{32,8},{40,16},{48,24},{56,32},{64,40},{72,48},{80,56},{88,... | collective-permute-start | bytes 2359304 | tf_op jit(solution)/shard_map/ppermute | solution.py:19
  218.8 49.5 %collective-permute-start.6 = (bf16[2,256,768]{2,1,0:T(8,128)(2,1)S(1)}, bf16[2,256,768]{2,1,0:T(8,128)(2,1)S(1)}, u32[]{:S(2)}, u32[]{:S(2)}) collective-permute-start(bf16[2,256,768]{2,1,0:T(8,128)(2,1)S(1)} %pad_maximum_fusion), channel_id=1, source_target_pairs={{32,0},{40,8},{48,16},{56,24},{64,32},{72,40},{80,48},{88,56},{96,... | collective-permute-start | bytes 2359304 | tf_op jit(solution)/shard_map/ppermute | solution.py:19
  289.9 5.4 copy-start.6
  289.9 5.4 copy-start.7
  289.9 5.4 copy-start.8
  325.0 5.6 copy-start.2
  325.0 7.3 copy-start.9
  325.0 9.3 %slice-start = ((s8[5308416]{0:T(1024)(128)(4,1)}), s8[4194304]{0:T(1024)(128)(4,1)S(1)}, s32[]{:S(2)}) async-start(s8[5308416]{0:T(1024)(128)(4,1)} %bitcast.221), calls=%async_computation.8 | async-start | bytes 8388608 | tf_op jit(solution)/shard_map/while
  332.3 2.1 slice-start.1
  334.4 6.7 copy-start.1
  441.1 5.6 copy-start.2
  441.1 7.3 copy-start.9
  441.1 9.3 %slice-start = ((s8[5308416]{0:T(1024)(128)(4,1)}), s8[4194304]{0:T(1024)(128)(4,1)S(1)}, s32[]{:S(2)}) async-start(s8[5308416]{0:T(1024)(128)(4,1)} %bitcast.221), calls=%async_computation.8 | async-start | bytes 8388608 | tf_op jit(solution)/shard_map/while
  448.4 2.1 slice-start.1
  450.5 6.7 copy-start.1
  553.6 5.0 copy-start
  579.1 9.3 %copy-start.3 = (f32[3,4,256,768]{3,2,1,0:T(8,128)S(1)}, f32[3,4,256,768]{3,2,1,0:T(8,128)}, u32[]{:S(2)}) copy-start(f32[3,4,256,768]{3,2,1,0:T(8,128)} %constant_dynamic-update-slice_fusion) | copy-start | bytes 28311556
  583.7 40.0 %copy-start.5 = (bf16[2,3,4,64,128]{4,3,2,1,0:T(8,128)(2,1)S(1)}, bf16[2,3,4,64,128]{4,3,2,1,0:T(8,128)(2,1)}, u32[]{:S(2)}) copy-start(bf16[2,3,4,64,128]{4,3,2,1,0:T(8,128)(2,1)} %get-tuple-element.250) | copy-start | bytes 1179652
  583.7 129.4 %collective-permute-start.9 = (f32[2,256,768]{2,1,0:T(8,128)}, f32[2,256,768]{2,1,0:T(8,128)}, u32[]{:S(2)}, u32[]{:S(2)}) collective-permute-start(f32[2,256,768]{2,1,0:T(8,128)} %get-tuple-element.338), channel_id=1, source_target_pairs={{32,0},{40,8},{48,16},{56,24},{64,32},{72,40},{80,48},{88,56},{96,... | collective-permute-start | bytes 4718600 | tf_op jit(solution)/shard_map/ppermute | solution.py:19
  590.3 119.4 %collective-permute-start.8 = (f32[1,256,768]{2,1,0:T(8,128)}, f32[1,256,768]{2,1,0:T(8,128)}, u32[]{:S(2)}, u32[]{:S(2)}) collective-permute-start(f32[1,256,768]{2,1,0:T(8,128)} %get-tuple-element.336), channel_id=1, source_target_pairs={{40,0},{48,8},{56,16},{64,24},{72,32},{80,40},{88,48},{96,56},{104... | collective-permute-start | bytes 2359304 | tf_op jit(solution)/shard_map/ppermute | solution.py:19
  607.7 109.0 %collective-permute-start.10 = (f32[1,256,768]{2,1,0:T(8,128)}, f32[1,256,768]{2,1,0:T(8,128)}, u32[]{:S(2)}, u32[]{:S(2)}) collective-permute-start(f32[1,256,768]{2,1,0:T(8,128)} %get-tuple-element.335), channel_id=1, source_target_pairs={{24,0},{32,8},{40,16},{48,24},{56,32},{64,40},{72,48},{80,56},{88,... | collective-permute-start | bytes 2359304 | tf_op jit(solution)/shard_map/ppermute | solution.py:19
  619.7 165.1 %collective-permute-start.11 = (f32[1,256,768]{2,1,0:T(8,128)}, f32[1,256,768]{2,1,0:T(8,128)}, u32[]{:S(2)}, u32[]{:S(2)}) collective-permute-start(f32[1,256,768]{2,1,0:T(8,128)} %get-tuple-element.334), channel_id=1, source_target_pairs={{8,0},{16,8},{24,16},{32,24},{40,32},{48,40},{56,48},{64,56},{72,6... | collective-permute-start | bytes 2359304 | tf_op jit(solution)/shard_map/ppermute | solution.py:19
  621.6 192.2 %collective-permute-start.14 = (f32[2,256,768]{2,1,0:T(8,128)}, f32[2,256,768]{2,1,0:T(8,128)}, u32[]{:S(2)}, u32[]{:S(2)}) collective-permute-start(f32[2,256,768]{2,1,0:T(8,128)} %get-tuple-element.337), channel_id=1, source_target_pairs={{0,32},{8,40},{16,48},{24,56},{32,64},{40,72},{48,80},{56,88},{64,... | collective-permute-start | bytes 4718600 | tf_op jit(solution)/shard_map/ppermute | solution.py:19
  625.2 190.3 %all-to-all-start.5 = ((bf16[8,64,384]{2,1,0:T(8,128)(2,1)}), bf16[8,64,384]{2,1,0:T(8,128)(2,1)S(1)}, u32[]{:S(2)}, u32[]{:S(2)}) async-start(bf16[8,64,384]{2,1,0:T(8,128)(2,1)} %all_to_all.120), calls=%async_computation.5 | async-start | bytes 786432 | tf_op jit(solution)/shard_map/all_to_all | solution.py:178
  635.2 81.5 %copy-start.4 = (f32[1,256,768]{2,1,0:T(8,128)S(1)}, f32[1,256,768]{2,1,0:T(8,128)}, u32[]{:S(2)}) copy-start(f32[1,256,768]{2,1,0:T(8,128)} %get-tuple-element.332) | copy-start | bytes 2359300
  709.8 76.3 %collective-permute-start.12 = (f32[1,256,768]{2,1,0:T(8,128)}, f32[1,256,768]{2,1,0:T(8,128)S(1)}, u32[]{:S(2)}, u32[]{:S(2)}) collective-permute-start(f32[1,256,768]{2,1,0:T(8,128)} %get-tuple-element.333), channel_id=1, source_target_pairs={{0,8},{8,16},{16,24},{24,32},{32,40},{40,48},{48,56},{56,64},{64,7... | collective-permute-start | bytes 2359304 | tf_op jit(solution)/shard_map/ppermute | solution.py:19
  713.1 160.1 %collective-permute-start.15 = (f32[1,256,768]{2,1,0:T(8,128)S(1)}, f32[1,256,768]{2,1,0:T(8,128)}, u32[]{:S(2)}, u32[]{:S(2)}) collective-permute-start(f32[1,256,768]{2,1,0:T(8,128)S(1)} %get-tuple-element.331), channel_id=1, source_target_pairs={{0,40},{8,48},{16,56},{24,64},{32,72},{40,80},{48,88},{56,96},{64,... | collective-permute-start | bytes 2359304 | tf_op jit(solution)/shard_map/ppermute | solution.py:19
  716.7 97.0 %collective-permute-start.13 = (f32[1,256,768]{2,1,0:T(8,128)S(1)}, f32[1,256,768]{2,1,0:T(8,128)S(1)}, u32[]{:S(2)}, u32[]{:S(2)}) collective-permute-start(f32[1,256,768]{2,1,0:T(8,128)S(1)} %copy-done.4), channel_id=1, source_target_pairs={{0,24},{8,32},{16,40},{24,48},{32,56},{40,64},{48,72},{56,80},{64,... | collective-permute-start | bytes 2359304 | tf_op jit(solution)/shard_map/ppermute | solution.py:19
  815.5 60.0 %all-to-all-start.4 = ((bf16[8,64,384]{2,1,0:T(8,128)(2,1)}), bf16[8,64,384]{2,1,0:T(8,128)(2,1)S(1)}, u32[]{:S(2)}, u32[]{:S(2)}) async-start(bf16[8,64,384]{2,1,0:T(8,128)(2,1)} %all_to_all.116), calls=%async_computation.4 | async-start | bytes 786432 | tf_op jit(solution)/shard_map/all_to_all | solution.py:177
  893.5 12.3 %all-to-all-start.7 = ((bf16[8,64,384]{2,1,0:T(8,128)(2,1)}), bf16[8,64,384]{2,1,0:T(8,128)(2,1)S(1)}, u32[]{:S(2)}, u32[]{:S(2)}) async-start(bf16[8,64,384]{2,1,0:T(8,128)(2,1)} %bitcast.61), calls=%async_computation.7 | async-start | bytes 786432 | tf_op jit(solution)/shard_map/all_to_all | solution.py:180
where the time goes:
time: 915 us; the launch traced here: 907 us
  waiting for transfers between devices  368 us (40%)
  local copies, waits for them, and re-layouts  173 us (19%)
  starting transfers between devices  155 us (17%)
  other arithmetic  135 us (15%)
  matrix products  48.3 us (5%)
  blocking collectives  18 us (2%)
    ppermute x16, waiting for transfers between devices, from_behind(): return lax.ppermute(value, axis, pairs)  347 us
    ppermute x16, starting transfers between devices, from_behind(): return lax.ppermute(value, axis, pairs)  109 us
    scatter-add x2, other arithmetic, one_block(): grad_kp = grad_kp.at[:, where_to].add(grad_k)  56.9 us
    scatter-add x2, other arithmetic, one_block(): grad_vp = grad_vp.at[:, where_to].add(grad_v)  56.7 us
    gather x4, local copies, waits for them, and re-layouts, attend_block(): key_pool[:, flat_slots].reshape(heads, count, WINDOW * TILE, HEAD_DIM)  23.8 us
    gather x4, local copies, waits for them, and re-layouts, attend_block(): value_pool[:, flat_slots].reshape(heads, count, WINDOW * TILE, HEAD_DIM)  20.2 us
  transfers between devices with their start and end apart: 23, of which 11 were waited for; matrix products, arithmetic and copies ran while one was open for 5% of the time, Pallas kernels for 0%

commit v1 on v0

v1 whole, which is shorter than its diff:
```python
import functools
import math

import jax
import jax.numpy as jnp
from jax import lax
from jax.experimental import pallas as pl
from jax.experimental.pallas import tpu as pltpu
from jax.sharding import PartitionSpec as P

HEADS = 24
HEAD_DIM = 128
D = HEADS * HEAD_DIM
TILE = 64
TLAYERS = 8
NH = 8
TW = 4
NX = 4
NZ = 8
NM = 8
NEG = -1e30
SCALE = 1.0 / math.sqrt(HEAD_DIM)
EXP2_SCALE = SCALE / math.log(2.0)
MESH = pl.DeviceIdType.MESH
BF16 = jnp.bfloat16
F32 = jnp.float32


def place():
    seat = lax.axis_index("seq")
    m = lax.axis_index("mp")
    x = seat // NZ
    z = lax.rem(seat, NZ)
    return x, z, m


def worker_of(part, head):
    rest_a = head - 8
    z_a = jnp.where(
        head < 8, 3 + 4 * lax.rem(head, 2), 2 + lax.rem(rest_a + 8, 2) + 4 * (lax.rem(rest_a + 8, 4) // 2)
    )
    m_a = jnp.where(head < 8, head // 2, 2 + head // 4)
    z_b = jnp.where(head < 16, lax.rem(head, 2) + 4 * (lax.rem(head, 4) // 2), 4 * lax.rem(head, 2))
    m_b = jnp.where(head < 16, head // 4, head // 2 - 4)
    return jnp.where(part == 0, z_a, z_b), jnp.where(part == 0, m_a, m_b)


def work_of(z, m):
    zq = lax.rem(z, 4)
    zh = z // 4
    part = jnp.where(zq >= 2, 0, 1)
    head_a = jnp.where(m < 4, 2 * m + zh, 4 * m - 8 + 2 * zh + (zq - 2))
    head_b = jnp.where(m < 4, 4 * m + 2 * zh + zq, 2 * m + 8 + zh)
    active = jnp.where(m < 4, zq != 2, zq != 1)
    return part, jnp.where(part == 0, head_a, head_b), active


def greet_plane(x, z, m):
    barrier = pltpu.get_barrier_semaphore()

    def greet(i, carry):
        zz = i // NM
        mm = lax.rem(i, NM)

        @pl.when(jnp.logical_or(zz != z, mm != m))
        def _():
            pl.semaphore_signal(barrier, inc=1, device_id=(x * NZ + zz, mm), device_id_type=MESH)

        return carry

    lax.fori_loop(0, NZ * NM, greet, 0)

    @pl.when(x > 0)
    def _():
        pl.semaphore_signal(barrier, inc=1, device_id=((x - 1) * NZ + z, m), device_id_type=MESH)

    @pl.when(x < NX - 1)
    def _():
        pl.semaphore_signal(barrier, inc=1, device_id=((x + 1) * NZ + z, m), device_id_type=MESH)

    peers = NZ * NM - 1 + jnp.where(x > 0, 1, 0) + jnp.where(x < NX - 1, 1, 0)
    pl.semaphore_wait(barrier, peers)


def wait_for(ref, sem):
    pltpu.make_async_copy(ref, ref, sem).wait()


def spread_kernel(
    q_ref, k_ref, v_ref, g_ref, flag_ref,
    qg_out, pool_out, flag_out,
    blank, send_sem, extra_sem, flag_send, kv_sem, qg_sem, flag_sem, halo_send, halo_sem, blank_sem,
):
    x, z, m = place()
    zh = z // 4
    zl = lax.rem(z, 4)
    h = 2 * zl + m // 4
    w = lax.rem(m, 4)
    own = zl // 2
    part, _, active = work_of(z, m)
    row0 = jnp.where(part == 0, 1, 0)
    blank[...] = jnp.zeros_like(blank)
    greet_plane(x, z, m)

    unused = jnp.where(part == 0, 0, 5)
    for layer in range(4):
        pltpu.make_async_copy(blank, pool_out.at[layer, pl.ds(unused, 1)], blank_sem.at[layer]).start()

    def blank_layer(layer, begin):
        copies = [
            pltpu.make_async_copy(blank, pool_out.at[layer, pl.ds(row0 + r, 1)], blank_sem.at[4 + r])
            for r in range(5)
        ]
        for c in copies:
            c.start() if begin else c.wait()

    @pl.when(x == 0)
    def _():
        blank_layer(0, True)

    @pl.when(x == NX - 1)
    def _():
        blank_layer(3, True)

    first = lax.rem(m * 3 + z * 5, HEADS)
    two = jnp.logical_or(h == 3, h == 4)
    other_row = jnp.where(h == 3, 0, 5)
    own_row = lax.rem(h, 4) + 1
    half = pl.ds(pl.multiple_of(lax.rem(w, 2) * TILE, TILE), TILE)

    def send_kv(j, carry):
        head = lax.rem(j + first, HEADS)
        columns = pl.ds(pl.multiple_of(head * HEAD_DIM, HEAD_DIM), HEAD_DIM)
        wz, wm = worker_of(own, head)
        for i, ref in ((0, k_ref), (1, v_ref)):
            pltpu.make_async_remote_copy(
                src_ref=ref.at[:, columns],
                dst_ref=pool_out.at[1 + zh, own_row, i, w // 2, half, :],
                send_sem=send_sem.at[i],
                recv_sem=kv_sem.at[zh, own_row],
                device_id=(x * NZ + wz, wm),
                device_id_type=MESH,
            ).start()

        @pl.when(two)
        def _():
            oz, om = worker_of(1 - own, head)
            for i, ref in ((0, k_ref), (1, v_ref)):
                pltpu.make_async_remote_copy(
                    src_ref=ref.at[:, columns],
                    dst_ref=pool_out.at[1 + zh, other_row, i, w // 2, half, :],
                    send_sem=extra_sem.at[i],
                    recv_sem=kv_sem.at[zh, other_row],
                    device_id=(x * NZ + oz, om),
                    device_id_type=MESH,
                ).start()

        return carry

    lax.fori_loop(0, HEADS, send_kv, 0)

    def send_flags(j, carry):
        wz, wm = worker_of(own, m * 3 + j)
        pltpu.make_async_remote_copy(
            src_ref=flag_ref.at[0],
            dst_ref=flag_out.at[zh, lax.rem(zl, 2)],
            send_sem=flag_send.at[j],
            recv_sem=flag_sem.at[zh, lax.rem(zl, 2)],
            device_id=(x * NZ + wz, wm),
            device_id_type=MESH,
        ).start()
        return carry

    lax.fori_loop(0, 3, send_flags, 0)

    def send_qg(j, carry):
        head = lax.rem(j + first, HEADS)
        columns = pl.ds(pl.multiple_of(head * HEAD_DIM, HEAD_DIM), HEAD_DIM)
        wz, wm = worker_of(own, head)
        for i, ref in ((0, q_ref), (1, g_ref)):
            pltpu.make_async_remote_copy(
                src_ref=ref.at[:, columns],
                dst_ref=qg_out.at[i, zh, lax.rem(h, 4), pl.ds(pl.multiple_of(w * TILE, TILE), TILE), :],
                send_sem=send_sem.at[2 + i],
                recv_sem=qg_sem,
                device_id=(x * NZ + wz, wm),
                device_id_type=MESH,
            ).start()
        return carry

    lax.fori_loop(0, HEADS, send_qg, 0)

    @pl.when(active)
    def _():
        def forward(r, carry):
            row = row0 + r
            wait_for(pool_out.at[1, row], kv_sem.at[0, row])

            @pl.when(x > 0)
            def _():
                pltpu.make_async_remote_copy(
                    src_ref=pool_out.at[1, row],
                    dst_ref=pool_out.at[3, row],
                    send_sem=halo_send.at[0],
                    recv_sem=halo_sem.at[1],
                    device_id=((x - 1) * NZ + z, m),
                    device_id_type=MESH,
                ).start()

            wait_for(pool_out.at[2, row], kv_sem.at[1, row])

            @pl.when(x < NX - 1)
            def _():
                pltpu.make_async_remote_copy(
                    src_ref=pool_out.at[2, row],
                    dst_ref=pool_out.at[0, row],
                    send_sem=halo_send.at[1],
                    recv_sem=halo_sem.at[0],
                    device_id=((x + 1) * NZ + z, m),
                    device_id_type=MESH,
                ).start()

            return carry

        lax.fori_loop(0, 5, forward, 0)
        wait_for(qg_out, qg_sem)
        for a in range(2):
            for b in range(2):
                wait_for(flag_out.at[a, b], flag_sem.at[a, b])

        @pl.when(x > 0)
        def _():
            wait_for(pool_out.at[1, pl.ds(row0, 5)], halo_send.at[0])
            wait_for(pool_out.at[0, pl.ds(row0, 5)], halo_sem.at[0])

        @pl.when(x < NX - 1)
        def _():
            wait_for(pool_out.at[2, pl.ds(row0, 5)], halo_send.at[1])
            wait_for(pool_out.at[3, pl.ds(row0, 5)], halo_sem.at[1])

    for i, ref in enumerate((k_ref, v_ref, q_ref, g_ref)):
        wait_for(ref, send_sem.at[i])

    @pl.when(two)
    def _():
        wait_for(k_ref, extra_sem.at[0])
        wait_for(v_ref, extra_sem.at[1])

    for j in range(3):
        wait_for(flag_ref.at[0], flag_send.at[j])
    for layer in range(4):
        pltpu.make_async_copy(blank, pool_out.at[layer, pl.ds(unused, 1)], blank_sem.at[layer]).wait()

    @pl.when(x == 0)
    def _():
        blank_layer(0, False)

    @pl.when(x == NX - 1)
    def _():
        blank_layer(3, False)


def spread(q, k, v, g, flags):
    any_space = pl.BlockSpec(memory_space=pl.ANY)
    return pl.pallas_call(
        spread_kernel,
        out_shape=(
            jax.ShapeDtypeStruct((2, 2, 4, 4 * TILE, HEAD_DIM), BF16),
            jax.ShapeDtypeStruct((4, 6, 2, 2, 2 * TILE, HEAD_DIM), BF16),
            jax.ShapeDtypeStruct((2, 2, 8, 128), F32),
        ),
        in_specs=[any_space] * 5,
        out_specs=(any_space,) * 3,
        scratch_shapes=[
            pltpu.VMEM((1, 2, 2, 2 * TILE, HEAD_DIM), BF16),
            pltpu.SemaphoreType.DMA((4,)),
            pltpu.SemaphoreType.DMA((2,)),
            pltpu.SemaphoreType.DMA((3,)),
            pltpu.SemaphoreType.DMA((2, 6)),
            pltpu.SemaphoreType.DMA,
            pltpu.SemaphoreType.DMA((2, 2)),
            pltpu.SemaphoreType.DMA((2,)),
            pltpu.SemaphoreType.DMA((2,)),
            pltpu.SemaphoreType.DMA((9,)),
        ],
        compiler_params=pltpu.CompilerParams(collective_id=0, has_side_effects=True),
        name="spread",
    )(q, k, v, g, flags)


def dot(a, b, dims):
    return lax.dot_general(a, b, (dims, ((), ())), preferred_element_type=F32)


def attend_kernel(qg_ref, pool_ref, flag_ref, place_ref, valid_ref, out_ref, mid_ref, halo_ref, acc):
    acc[...] = jnp.zeros_like(acc)

    def strip(s, carry):
        zh = s // 4
        r = lax.rem(s, 4)
        q = qg_ref[0, zh, r]
        g = qg_ref[1, zh, r]
        flags = flag_ref[zh, r // 2].astype(BF16)
        odd = lax.rem(r, 2) == 1
        scores, keys, values = [], [], []
        for pair in range(2):
            rows = slice(pair * TILE, pair * TILE + 3 * TILE)
            key = [pool_ref[zh + a, pl.ds(r, 3), 0, pair].reshape(384, HEAD_DIM) for a in range(3)]
            value = [pool_ref[zh + a, pl.ds(r, 3), 1, pair].reshape(384, HEAD_DIM) for a in range(3)]
            keys.append(jnp.concatenate(key, axis=0))
            values.append(jnp.concatenate(value, axis=0))
            live = dot(flags, place_ref[pair], ((1,), (0,)))
            live = jnp.where(odd, live[4:8], live[0:4])
            ok = jnp.concatenate(
                [valid_ref[zh + a, r + b, pair : pair + 1] for a in range(3) for b in range(3)], axis=1
            )
            bias = (live * ok - 1.0) * (-NEG)
            bias = jnp.concatenate(
                [jnp.broadcast_to(bias[pair + j : pair + j + 1], (TILE, 1152)) for j in range(3)], axis=0
            )
            scores.append(dot(q[rows], keys[pair], ((1,), (1,))) + bias)
        tops = [jnp.max(sc, axis=1, keepdims=True) for sc in scores]
        middle = jnp.maximum(tops[0][TILE:], tops[1][: 2 * TILE])
        top0 = jnp.concatenate([tops[0][:TILE], middle], axis=0)
        top1 = jnp.concatenate([middle, tops[1][2 * TILE :]], axis=0)
        expo = [jnp.exp2((sc - t) * EXP2_SCALE) for sc, t in zip(scores, (top0, top1))]
        sums = [jnp.sum(e, axis=1, keepdims=True) for e in expo]
        middle = sums[0][TILE:] + sums[1][: 2 * TILE]
        inv0 = 1.0 / jnp.concatenate([sums[0][:TILE], middle], axis=0)
        inv1 = 1.0 / jnp.concatenate([middle, sums[1][2 * TILE :]], axis=0)
        probs = [expo[0] * inv0, expo[1] * inv1]
        low = [p.astype(BF16) for p in probs]

        def join(a, b):
            return jnp.concatenate([a[:TILE], a[TILE:] + b[: 2 * TILE], b[2 * TILE :]], axis=0)

        attended = join(*[dot(low[i], values[i], ((1,), (0,))) for i in range(2)]).astype(BF16)
        out_ref[0, zh, r] = attended
        delta = jnp.sum(g.astype(F32) * attended.astype(F32), axis=1, keepdims=True)
        grads = []
        for pair in range(2):
            rows = slice(pair * TILE, pair * TILE + 3 * TILE)
            dprobs = dot(g[rows], values[pair], ((1,), (1,)))
            dscores = (probs[pair] * (dprobs - delta[rows])).astype(BF16)
            grads.append(dot(dscores, keys[pair], ((1,), (0,))))
            grad_k = dot(dscores, q[rows], ((0,), (0,))).reshape(3, 3, 2 * TILE, HEAD_DIM)
            grad_v = dot(low[pair], g[rows], ((0,), (0,))).reshape(3, 3, 2 * TILE, HEAD_DIM)
            for a in range(3):
                acc[zh + a, pl.ds(r, 3), 0, pair] += grad_k[a]
                acc[zh + a, pl.ds(r, 3), 1, pair] += grad_v[a]
        out_ref[1, zh, r] = (join(*grads) * SCALE).astype(BF16)
        return carry

    lax.fori_loop(0, 8, strip, 0)
    for i, factor in ((0, SCALE), (1, 1.0)):
        mid_ref[:, :, i] = acc[1:3, :, i] * factor
        halo_ref[0, :, i] = (acc[0, :, i] * factor).astype(BF16)
        halo_ref[1, :, i] = (acc[3, :, i] * factor).astype(BF16)


def attend(qg, pool, flags, places, valid):
    vmem = pl.BlockSpec(memory_space=pltpu.VMEM)
    return pl.pallas_call(
        attend_kernel,
        out_shape=(
            jax.ShapeDtypeStruct((2, 2, 4, 4 * TILE, HEAD_DIM), BF16),
            jax.ShapeDtypeStruct((2, 6, 2, 2, 2 * TILE, HEAD_DIM), F32),
            jax.ShapeDtypeStruct((2, 6, 2, 2, 2 * TILE, HEAD_DIM), BF16),
        ),
        in_specs=[vmem] * 5,
        out_specs=(vmem,) * 3,
        scratch_shapes=[pltpu.VMEM((4, 6, 2, 2, 2 * TILE, HEAD_DIM), F32)],
        compiler_params=pltpu.CompilerParams(vmem_limit_bytes=56 * 1024 * 1024),
        cost_estimate=pl.CostEstimate(flops=5_400_000_000, bytes_accessed=14_000_000, transcendentals=3_600_000),
        name="attend",
    )(qg, pool, flags, places, valid)


def collect_kernel(
    out_ref, mid_ref, halo_ref,
    token_out, extra_out,
    came, total, send_sem, kv_send, halo_send, halo_sem, token_sem, extra_sem,
):
    x, z, m = place()
    zl = lax.rem(z, 4)
    h = 2 * zl + m // 4
    part, head, active = work_of(z, m)
    row0 = jnp.where(part == 0, 1, 0)
    two = jnp.logical_or(h == 3, h == 4)
    columns = pl.ds(pl.multiple_of(head * HEAD_DIM, HEAD_DIM), HEAD_DIM)
    greet_plane(x, z, m)

    @pl.when(active)
    def _():
        def send_halo(r, carry):
            row = row0 + r

            @pl.when(x > 0)
            def _():
                pltpu.make_async_remote_copy(
                    src_ref=halo_ref.at[0, row],
                    dst_ref=came.at[1, row],
                    send_sem=halo_send.at[0],
                    recv_sem=halo_sem.at[1, row],
                    device_id=((x - 1) * NZ + z, m),
                    device_id_type=MESH,
                ).start()

            @pl.when(x < NX - 1)
            def _():
                pltpu.make_async_remote_copy(
                    src_ref=halo_ref.at[1, row],
                    dst_ref=came.at[0, row],
                    send_sem=halo_send.at[1],
                    recv_sem=halo_sem.at[0, row],
                    device_id=((x + 1) * NZ + z, m),
                    device_id_type=MESH,
                ).start()

            return carry

        lax.fori_loop(0, 5, send_halo, 0)

        def send_tokens(j, carry):
            j = lax.rem(j + head, 32)
            layer = j // 16
            r = lax.rem(j // 4, 4)
            w = lax.rem(j, 4)
            there = part * 4 + r
            oz = layer * 4 + there // 2
            om = lax.rem(there, 2) * 4 + w
            for i in range(2):
                pltpu.make_async_remote_copy(
                    src_ref=out_ref.at[i, layer, r, pl.ds(pl.multiple_of(w * TILE, TILE), TILE), :],
                    dst_ref=token_out.at[i, :, columns],
                    send_sem=send_sem,
                    recv_sem=token_sem.at[i],
                    device_id=(x * NZ + oz, om),
                    device_id_type=MESH,
                ).start()
            return carry

        lax.fori_loop(0, 32, send_tokens, 0)

        def send_grads(j, carry):
            layer = j // 5
            row = row0 + lax.rem(j, 5)
            there = part * 4 + row - 1
            here = jnp.where(layer == 0, x > 0, x < NX - 1)

            @pl.when(here)
            def _():
                wait_for(came.at[layer, row], halo_sem.at[layer, row])
                total[layer, row] = (mid_ref[layer, row] + came[layer, row].astype(F32)).astype(BF16)

            @pl.when(jnp.logical_not(here))
            def _():
                total[layer, row] = mid_ref[layer, row].astype(BF16)

            oz = layer * 4 + there // 2
            mine = there // 4 == part

            def send(w, carry):
                om = lax.rem(there, 2) * 4 + w
                half = pl.ds(pl.multiple_of(lax.rem(w, 2) * TILE, TILE), TILE)

                for i in range(2):
                    @pl.when(mine)
                    def _():
                        pltpu.make_async_remote_copy(
                            src_ref=total.at[layer, row, i, w // 2, half, :],
                            dst_ref=token_out.at[2 + i, :, columns],
                            send_sem=kv_send,
                            recv_sem=token_sem.at[2 + i],
                            device_id=(x * NZ + oz, om),
                            device_id_type=MESH,
                        ).start()

                    @pl.when(jnp.logical_not(mine))
                    def _():
                        pltpu.make_async_remote_copy(
                            src_ref=total.at[layer, row, i, w // 2, half, :],
                            dst_ref=extra_out.at[i, :, columns],
                            send_sem=kv_send,
                            recv_sem=extra_sem.at[i],
                            device_id=(x * NZ + oz, om),
                            device_id_type=MESH,
                        ).start()

                return carry

            return lax.fori_loop(0, 4, send, carry)

        lax.fori_loop(0, 10, send_grads, 0)
        wait_for(out_ref, send_sem)
        wait_for(total.at[:, pl.ds(row0, 5)], kv_send)

        @pl.when(x > 0)
        def _():
            wait_for(halo_ref.at[0, pl.ds(row0, 5)], halo_send.at[0])

        @pl.when(x < NX - 1)
        def _():
            wait_for(halo_ref.at[1, pl.ds(row0, 5)], halo_send.at[1])

    for i in range(4):
        wait_for(token_out.at[i], token_sem.at[i])

    @pl.when(two)
    def _():
        for i in range(2):
            wait_for(extra_out.at[i], extra_sem.at[i])


def collect(out, mid, halo):
    any_space = pl.BlockSpec(memory_space=pl.ANY)
    vmem = pl.BlockSpec(memory_space=pltpu.VMEM)
    shape = (2, 6, 2, 2, 2 * TILE, HEAD_DIM)
    return pl.pallas_call(
        collect_kernel,
        out_shape=(
            jax.ShapeDtypeStruct((4, TILE, D), BF16),
            jax.ShapeDtypeStruct((2, TILE, D), BF16),
        ),
        in_specs=[any_space, vmem, any_space],
        out_specs=(any_space,) * 2,
        scratch_shapes=[
            pltpu.VMEM(shape, BF16),
            pltpu.VMEM(shape, BF16),
            pltpu.SemaphoreType.DMA,
            pltpu.SemaphoreType.DMA,
            pltpu.SemaphoreType.DMA((2,)),
            pltpu.SemaphoreType.DMA((2, 6)),
            pltpu.SemaphoreType.DMA((4,)),
            pltpu.SemaphoreType.DMA((2,)),
        ],
        compiler_params=pltpu.CompilerParams(
            collective_id=1, has_side_effects=True, vmem_limit_bytes=32 * 1024 * 1024
        ),
        name="collect",
    )(out, mid, halo)


def on_device(queries, keys, values, out_grad, window_lists, valid_counts):
    x, z, m = place()
    zl = lax.rem(z, 4)
    t = 2 * x + z // 4
    h = 2 * zl + m // 4
    w = lax.rem(m, 4)
    part, _, _ = work_of(z, m)
    count = lax.dynamic_index_in_dim(valid_counts, (t * NH + h) * TW + w, keepdims=False)
    valid = jnp.arange(TILE, dtype=jnp.int32)[:, None] < count
    cot = jnp.where(valid, out_grad, jnp.zeros_like(out_grad))

    spot = jnp.arange(128, dtype=jnp.int32)[None, :]
    mine = jnp.arange(8, dtype=jnp.int32)[:, None]
    near_t = t + spot // 12 - 1
    near_h = 2 * zl + mine // 4 + spot // 4 % 3 - 1
    near = (near_t * NH + near_h) * TW + spot % 4
    inside = (spot < 36) & (near_t >= 0) & (near_t < TLAYERS) & (near_h >= 0) & (near_h < NH)
    listed = jnp.any(window_lists[:, :, None] == near[:, None, :], axis=1)
    flags = (inside & listed).astype(F32)[None]

    counts = jnp.pad(valid_counts.reshape(TLAYERS, NH, TW), ((1, 1), (1, 1), (0, 0)))
    counts = lax.dynamic_slice(counts, (2 * x, 4 * part, 0), (4, 6, TW))
    key_ok = jnp.arange(TILE, dtype=jnp.int32) < counts[..., None]
    key_ok = key_ok.astype(F32).reshape(4, 6, 2, 2 * TILE)

    key = jnp.arange(1152, dtype=jnp.int32)[None, None, :]
    pair = jnp.arange(2, dtype=jnp.int32)[:, None, None]
    wanted = key // 128 * 4 + pair * 2 + key % 128 // TILE
    places = (wanted == jnp.arange(128, dtype=jnp.int32)[None, :, None]).astype(BF16)

    qg, pool, flag_pool = spread(queries, keys, values, cot, flags)
    out, mid, halo = attend(qg, pool, flag_pool, places, key_ok)
    tokens, extra = collect(out, mid, halo)
    attended = jnp.where(valid, tokens[0], jnp.zeros_like(tokens[0]))
    two = jnp.logical_or(h == 3, h == 4)

    def joined(a, b):
        return jnp.where(two, (a.astype(F32) + b.astype(F32)).astype(BF16), a)

    return attended, tokens[1], joined(tokens[2], extra[0]), joined(tokens[3], extra[1])


def solution(mesh):
    rows = P(("seq", "mp"), None)
    return jax.shard_map(
        on_device,
        mesh=mesh,
        in_specs=(rows, rows, rows, rows, P("seq", None), P()),
        out_specs=(rows, rows, rows, rows),
        check_vma=False,
    )
```

time: 915 us -> 171 us (0.19)
  the two profiles are of different devices: /device:TPU:68 before, /device:TPU:73 now
where the time goes in v1:
time: 171 us
  Pallas kernels  155 us (91%)
  local copies, waits for them, and re-layouts  8.39 us (5%)
  other arithmetic  6.19 us (4%)
    pallas_call x1, Pallas kernels, collect(): pl.pallas_call(collect_kernel, out_shape=(jax.ShapeDtypeStruct((4, TILE,...  72 us
    pallas_call x1, Pallas kernels, spread(): pl.pallas_call(spread_kernel, out_shape=(jax.ShapeDtypeStruct((2, 2, 4, 4...  56.7 us
    pallas_call x1, Pallas kernels, attend(): pl.pallas_call(attend_kernel, out_shape=(jax.ShapeDtypeStruct((2, 2, 4, 4...  26.5 us
    unnamed x7, local copies, waits for them, and re-layouts  5.29 us

profile of v1, /device:TPU:73, one launch (start us, length us, event | category | flops | bytes accessed | tf_op | source)
XLA Modules:
  0.0 170.6 jit_solution(7562527375532107101)
XLA Ops:
  0.7 1.3 dynamic_slice.7
  2.0 0.6 iota_compare_fusion.1
  2.7 0.1 lt.103
  2.8 0.1 multiply_add_fusion
  2.9 0.8 copy.10
  3.6 0.1 compare_reduce_fusion
  3.7 0.7 fusion.23.flag_ref
  4.4 0.1 add_add_fusion
  4.5 0.8 reshape.442
  5.3 0.1 lt.107
  5.4 0.1 lt.108
  5.5 0.6 compare_convert_fusion.valid_ref
  6.1 1.8 %broadcast_select_fusion.g_ref = bf16[64,3072]{1,0:T(8,128)(2,1)} fusion(bf16[64,3072]{1,0:T(8,128)(2,1)} %param.9, pred[64]{0:T(512)(128)(4,1)S(1)} %iota_compare_fusion.1), kind=kLoop, calls=%fused_computation.10 | loop fusion | flops 196608 | bytes 786496 | tf_op jit(solution)/shard_map/jit(_where)/select_n | solution.py:553
  8.0 0.9 fusion.place_ref
  8.9 56.7 %spread.1 = (bf16[2,2,4,256,128]{4,3,2,1,0:T(8,128)(2,1)}, bf16[4,6,2,2,128,128]{5,4,3,2,1,0:T(8,128)(2,1)}, f32[2,2,8,128]{3,2,1,0:T(8,128)}) custom-call(bf16[64,3072]{1,0:T(8,128)(2,1)} %q_ref.1, bf16[64,3072]{1,0:T(8,128)(2,1)} %k_ref.1, bf16[64,3072]{1,0:T(8,128)(2,1)} %v_ref.1, bf16[64,3072]{1,0:T(8,128)(2,1)} %broadcast_select_fusion.g_ref, ...), custom_call_target="tpu_custom_call" | custom-call | tf_op jit(solution)/shard_map/spread/pallas_call | solution.py:265
  65.6 26.5 %attend.1 = (bf16[2,2,4,256,128]{4,3,2,1,0:T(8,128)(2,1)}, f32[2,6,2,2,128,128]{5,4,3,2,1,0:T(8,128)}, bf16[2,6,2,2,128,128]{5,4,3,2,1,0:T(8,128)(2,1)}) custom-call(bf16[2,2,4,256,128]{4,3,2,1,0:T(8,128)(2,1)} %get-tuple-element.12.qg_ref, bf16[4,6,2,2,128,128]{5,4,3,2,1,0:T(8,128)(2,1)} %get-tuple-element.13.pool_ref, ...), custom_call_target="tpu_custom_call" | custom-call | flops 5400000000 | bytes 14000000 | tf_op jit(solution)/shard_map/attend/pallas_call | solution.py:363
  92.1 0.0 copy-start
  92.1 1.9 %copy-done = f32[2,6,2,2,128,128]{5,4,3,2,1,0:T(8,128)S(1)} copy-done((f32[2,6,2,2,128,128]{5,4,3,2,1,0:T(8,128)S(1)}, f32[2,6,2,2,128,128]{5,4,3,2,1,0:T(8,128)}, u32[]{:S(2)}) %copy-start) | copy-done | bytes 3145752
  94.0 0.0 copy-start.1
  94.0 1.4 copy-done.1
  95.4 0.0 copy-start.2
  95.4 1.2 copy-done.2
  96.6 72.0 %collect.1 = (bf16[4,64,3072]{2,1,0:T(8,128)(2,1)S(1)}, bf16[2,64,3072]{2,1,0:T(8,128)(2,1)S(1)}) custom-call(bf16[2,2,4,256,128]{4,3,2,1,0:T(8,128)(2,1)S(1)} %copy-done.2, f32[2,6,2,2,128,128]{5,4,3,2,1,0:T(8,128)S(1)} %copy-done, bf16[2,6,2,2,128,128]{5,4,3,2,1,0:T(8,128)(2,1)S(1)} %copy-done.1), custom_call_target="tpu_custom_call" | custom-call | tf_op jit(solution)/shard_map/collect/pallas_call | solution.py:519
  168.6 1.2 fusion.4
  169.8 0.8 slice_bitcast_fusion
  (8 shorter events, 0.1 us)
Async XLA Ops:
  92.1 1.9 %copy-start = (f32[2,6,2,2,128,128]{5,4,3,2,1,0:T(8,128)S(1)}, f32[2,6,2,2,128,128]{5,4,3,2,1,0:T(8,128)}, u32[]{:S(2)}) copy-start(f32[2,6,2,2,128,128]{5,4,3,2,1,0:T(8,128)} %get-tuple-element.16.mid_ref) | copy-start | bytes 9437188
  94.0 1.4 copy-start.1
  95.4 1.2 copy-start.2

commit v2 on v0

v2 whole, which is shorter than its diff:
```python
import math

import jax
import jax.numpy as jnp
from jax import lax
from jax.experimental import pallas as pl
from jax.experimental.pallas import tpu as pltpu
from jax.sharding import PartitionSpec as P

HEADS = 24
HEAD_DIM = 128
D = HEADS * HEAD_DIM
TILE = 64
WINDOW = 27
TLAYERS = 8
NH = 8
TW = 4
TILES = TLAYERS * NH * TW
NX = 4
NZ = 8
NM = 8
WAVES = 3
KEYS = 9 * 2 * TILE
BIG = 1e30
SCALE = 1.0 / math.sqrt(HEAD_DIM)
EXP2_SCALE = SCALE / math.log(2.0)
MESH = pl.DeviceIdType.MESH
BF16 = jnp.bfloat16
F32 = jnp.float32


def place():
    seat = lax.axis_index("seq")
    m = lax.axis_index("mp")
    return seat // NZ, lax.rem(seat, NZ), m


def worker_z(part, m, wave):
    u = lax.rem(wave + m // 2, 2)
    v = lax.rem(m + wave // 2, 2)
    return jnp.where(part == 0, 3 - u + 4 * v, lax.rem(4 - 3 * u + 4 * v, NZ))


def work_of(z, m):
    zq = lax.rem(z, 4)
    zh = z // 4
    part = jnp.where(zq >= 2, 0, 1)
    u = jnp.where(part == 0, 3 - zq, zq)
    v = jnp.where(jnp.logical_and(part == 1, u == 0), 1 - zh, zh)
    same_v = v == lax.rem(m, 2)
    same_u = u == lax.rem(m // 2, 2)
    wave = jnp.where(same_u, jnp.where(same_v, 0, 2), 1)
    return part, wave, jnp.logical_or(same_u, same_v)


def greet_plane(x, z, m):
    barrier = pltpu.get_barrier_semaphore()

    def greet(i, carry):
        zz = i // NM
        mm = lax.rem(i, NM)

        @pl.when(jnp.logical_or(zz != z, mm != m))
        def _():
            pl.semaphore_signal(barrier, inc=1, device_id=(x * NZ + zz, mm), device_id_type=MESH)

        return carry

    lax.fori_loop(0, NZ * NM, greet, 0)

    @pl.when(x > 0)
    def _():
        pl.semaphore_signal(barrier, inc=1, device_id=((x - 1) * NZ + z, m), device_id_type=MESH)

    @pl.when(x < NX - 1)
    def _():
        pl.semaphore_signal(barrier, inc=1, device_id=((x + 1) * NZ + z, m), device_id_type=MESH)

    peers = NZ * NM - 1 + jnp.where(x > 0, 1, 0) + jnp.where(x < NX - 1, 1, 0)
    pl.semaphore_wait(barrier, peers)


def wait_for(ref, sem):
    pltpu.make_async_copy(ref, ref, sem).wait()


def send(src, dst, send_sem, recv_sem, seat, m):
    pltpu.make_async_remote_copy(
        src_ref=src, dst_ref=dst, send_sem=send_sem, recv_sem=recv_sem,
        device_id=(seat, m), device_id_type=MESH,
    ).start()


def dot(a, b, dims):
    return lax.dot_general(a, b, (dims, ((), ())), preferred_element_type=F32)


def tile_rows(w):
    return pl.ds(pl.multiple_of(w * TILE, TILE), TILE)


def head_columns(head):
    return pl.ds(pl.multiple_of(head * HEAD_DIM, HEAD_DIM), HEAD_DIM)


def kernel(
    q_ref, k_ref, v_ref, g_ref, list_ref, count_ref,
    att_out, gq_out, gk_out, gv_out,
    pool, qg, out, acc, edge, came, passed, total, flag_mine, flag_all, places, valid, bias,
    send_sem, kv_sem, qg_sem, flag_send, flag_sem, xsend, xsem, zsend, zsem,
    out_send, token_sem, edge_send, edge_sem, part_send, part_sem, total_send,
):
    x, z, m = place()
    zh = z // 4
    zl = lax.rem(z, 4)
    h = 2 * zl + m // 4
    w = lax.rem(m, 4)
    t = 2 * x + zh
    own = zl // 2
    part, wave, active = work_of(z, m)
    head = 3 * m + wave
    has_low = x > 0
    has_high = x < NX - 1
    low_seat = (x - 1) * NZ + z
    high_seat = (x + 1) * NZ + z
    other_seat = x * NZ + worker_z(1 - part, m, wave)

    spot = lax.broadcasted_iota(jnp.int32, (8, 128), 1)
    mine = lax.broadcasted_iota(jnp.int32, (8, 128), 0)
    near_t = t + spot // 12 - 1
    near_h = 2 * zl + mine // 4 + lax.rem(spot // 4, 3) - 1
    near = (near_t * NH + near_h) * TW + lax.rem(spot, 4)
    inside = (spot < 36) & (near_t >= 0) & (near_t < TLAYERS) & (near_h >= 0) & (near_h < NH)
    near = jnp.where(inside, near, -2)
    listed = jnp.zeros((8, 128), F32)
    for j in range(WINDOW):
        listed = jnp.where(list_ref[:, j : j + 1] == near, 1.0, listed)
    flag_mine[...] = listed
    pool[...] = jnp.zeros_like(pool)
    greet_plane(x, z, m)

    my_rows = tile_rows(lax.rem(w, 2))

    def send_wave(number, carry):
        def send_kv(j, carry):
            wm = lax.rem(j + m + z, NM)
            seat = x * NZ + worker_z(own, wm, number)
            columns = head_columns(3 * wm + number)
            row = lax.rem(h, 4)
            for i, ref in ((0, k_ref), (1, v_ref)):
                send(
                    ref.at[:, columns], pool.at[1 + zh, 1 + row, i, w // 2, my_rows, :],
                    send_sem.at[i], kv_sem.at[zh, row], seat, wm,
                )
            return carry

        def send_qg(j, carry):
            wm = lax.rem(j + m + z, NM)
            seat = x * NZ + worker_z(own, wm, number)
            columns = head_columns(3 * wm + number)
            row = lax.rem(h, 4)
            for i, ref in ((0, q_ref), (1, g_ref)):
                send(
                    ref.at[:, columns], qg.at[zh, row, i, tile_rows(w), :],
                    send_sem.at[2 + i], qg_sem.at[zh, row], seat, wm,
                )
            return carry

        lax.fori_loop(0, NM, send_kv, 0)
        send(
            flag_mine, flag_all.at[zh, lax.rem(zl, 2)],
            flag_send.at[number], flag_sem.at[zh, lax.rem(zl, 2)],
            x * NZ + worker_z(own, m, number), m,
        )
        lax.fori_loop(0, NM, send_qg, 0)
        return carry

    lax.fori_loop(0, WAVES, send_wave, 0)

    def row_of(i):
        return jnp.where(part == 0, 5 - i, i)

    def work():
        acc[...] = jnp.zeros_like(acc)
        lane = lax.broadcasted_iota(jnp.int32, (1, 128), 1)

        def mark(i, carry):
            layer = i // 6
            row = lax.rem(i, 6)
            key_t = 2 * x - 1 + layer
            key_h = 4 * part - 1 + row
            real = (key_t >= 0) & (key_t < TLAYERS) & (key_h >= 0) & (key_h < NH)
            first = jnp.where(real, (key_t * NH + key_h) * TW, 0)
            for pair in range(2):
                counts = [jnp.where(real, count_ref[first + 2 * pair + j], 0) for j in range(2)]
                until = jnp.where(lane < TILE, counts[0], counts[1] + TILE)
                valid[layer, row, pair : pair + 1, :] = jnp.where(lane < until, 1.0, 0.0)
            return carry

        lax.fori_loop(0, 24, mark, 0)

        key = lax.broadcasted_iota(jnp.int32, (128, KEYS), 1)
        flag = lax.broadcasted_iota(jnp.int32, (128, KEYS), 0)
        for pair in range(2):
            wanted = key // 128 * 4 + pair * 2 + lax.rem(key, 128) // TILE
            places[pair] = jnp.where(wanted == flag, 1.0, 0.0).astype(BF16)

        def forward(i, carry):
            row = row_of(i)
            for side in range(2):
                @pl.when(i > 0)
                def _():
                    wait_for(pool.at[1 + side, row], kv_sem.at[side, jnp.maximum(row, 1) - 1])

                @pl.when(i == 0)
                def _():
                    wait_for(pool.at[1 + side, row], zsem.at[side])

                @pl.when(i == 1)
                def _():
                    send(
                        pool.at[1 + side, row], pool.at[1 + side, jnp.where(part == 0, 0, 5)],
                        zsend.at[side], zsem.at[side], other_seat, m,
                    )

            @pl.when(has_low)
            def _():
                send(pool.at[1, row], pool.at[3, row], xsend.at[0], xsem.at[1, row], low_seat, m)

            @pl.when(has_high)
            def _():
                send(pool.at[2, row], pool.at[0, row], xsend.at[1], xsem.at[0, row], high_seat, m)

            return carry

        lax.fori_loop(1, 5, forward, 0)
        forward(0, 0)

        def make_bias(layer, carry):
            for a in range(2):
                wait_for(flag_all.at[layer, a], flag_sem.at[layer, a])
            for pair in range(2):
                for r in range(4):
                    if r % 2 == 0:
                        live = dot(flag_all[layer, r // 2].astype(BF16), places[pair], ((1,), (0,)))
                    ok = jnp.concatenate(
                        [valid[layer + a, r + b, pair : pair + 1, :] for a in range(3) for b in range(3)], axis=1
                    )
                    tiles = live[(r % 2) * 4 : (r % 2) * 4 + 4]
                    bias[layer, r, pair, 0:4, :] = (tiles * ok - 1.0) * BIG
            return carry

        lax.fori_loop(0, 2, make_bias, 0)

        def arrive(i, carry):
            row = row_of(i)

            @pl.when(has_low)
            def _():
                wait_for(pool.at[0, row], xsem.at[0, row])

            @pl.when(has_high)
            def _():
                wait_for(pool.at[3, row], xsem.at[1, row])

            return carry

        lax.fori_loop(0, 5, arrive, 0)

        position = lax.broadcasted_iota(jnp.int32, (TILE, HEAD_DIM), 0)

        def strip(layer, r):
            wait_for(qg.at[layer, r], qg_sem.at[layer, r])
            tile0 = ((2 * x + layer) * NH + 4 * part + r) * TW
            token_ok = jnp.concatenate([position < count_ref[tile0 + j] for j in range(TW)], axis=0)
            q = qg[layer, r, 0]
            g = qg[layer, r, 1]
            g = jnp.where(token_ok, g.astype(F32), 0.0).astype(BF16)
            scores, keys, values = [], [], []
            for pair in range(2):
                rows = slice(pair * TILE, pair * TILE + 3 * TILE)
                key = [pool[layer + a, pl.ds(r, 3), 0, pair].reshape(384, HEAD_DIM) for a in range(3)]
                value = [pool[layer + a, pl.ds(r, 3), 1, pair].reshape(384, HEAD_DIM) for a in range(3)]
                keys.append(jnp.concatenate(key, axis=0))
                values.append(jnp.concatenate(value, axis=0))
                out_of = jnp.concatenate(
                    [
                        jnp.broadcast_to(bias[layer, r, pair, pair + j : pair + j + 1, :], (TILE, KEYS))
                        for j in range(3)
                    ],
                    axis=0,
                )
                scores.append(dot(q[rows], keys[pair], ((1,), (1,))) + out_of)
            tops = [jnp.max(sc, axis=1, keepdims=True) for sc in scores]
            middle = jnp.maximum(tops[0][TILE:], tops[1][: 2 * TILE])
            top0 = jnp.concatenate([tops[0][:TILE], middle], axis=0)
            top1 = jnp.concatenate([middle, tops[1][2 * TILE :]], axis=0)
            expo = [jnp.exp2((sc - top) * EXP2_SCALE) for sc, top in zip(scores, (top0, top1))]
            sums = [jnp.sum(e, axis=1, keepdims=True) for e in expo]
            middle = sums[0][TILE:] + sums[1][: 2 * TILE]
            inv0 = 1.0 / jnp.concatenate([sums[0][:TILE], middle], axis=0)
            inv1 = 1.0 / jnp.concatenate([middle, sums[1][2 * TILE :]], axis=0)
            probs = [expo[0] * inv0, expo[1] * inv1]
            low = [p.astype(BF16) for p in probs]

            def join(a, b):
                return jnp.concatenate([a[:TILE], a[TILE:] + b[: 2 * TILE], b[2 * TILE :]], axis=0)

            attended = join(*[dot(low[i], values[i], ((1,), (0,))) for i in range(2)])
            attended = jnp.where(token_ok, attended, 0.0).astype(BF16)
            out[layer, r, 0] = attended
            delta = jnp.sum(g.astype(F32) * attended.astype(F32), axis=1, keepdims=True)
            grads = []
            for pair in range(2):
                rows = slice(pair * TILE, pair * TILE + 3 * TILE)
                dprobs = dot(g[rows], values[pair], ((1,), (1,)))
                dscores = (probs[pair] * (dprobs - delta[rows])).astype(BF16)
                grads.append(dot(dscores, keys[pair], ((1,), (0,))))
                grad_k = dot(dscores, q[rows], ((0,), (0,))).reshape(3, 3, 2 * TILE, HEAD_DIM)
                grad_v = dot(low[pair], g[rows], ((0,), (0,))).reshape(3, 3, 2 * TILE, HEAD_DIM)
                for a in range(3):
                    acc[layer + a, pl.ds(r, 3), 0, pair] += grad_k[a]
                    acc[layer + a, pl.ds(r, 3), 1, pair] += grad_v[a]
            out[layer, r, 1] = (join(*grads) * SCALE).astype(BF16)

        columns = head_columns(head)

        def seat_of(layer, row):
            return x * NZ + layer * 4 + (4 * part + row) // 2, lax.rem(row, 2) * 4

        def send_strip(layer, r):
            seat, m0 = seat_of(layer, r)

            def send_tile(j, carry):
                for i, ref in ((0, att_out), (1, gq_out)):
                    send(
                        out.at[layer, r, i, tile_rows(j), :], ref.at[:, columns],
                        out_send, token_sem.at[i], seat, m0 + j,
                    )
                return carry

            lax.fori_loop(0, TW, send_tile, 0)

        def scaled(layer, row, i):
            return acc[layer, row, i] * (SCALE if i == 0 else 1.0)

        def send_edge(i):
            row = row_of(i)

            @pl.when(has_low)
            def _():
                for j in range(2):
                    edge[0, i, j] = scaled(0, row, j).astype(BF16)
                send(edge.at[0, i], came.at[1, i], edge_send.at[0], edge_sem.at[1, i], low_seat, m)

            @pl.when(has_high)
            def _():
                for j in range(2):
                    edge[1, i, j] = scaled(3, row, j).astype(BF16)
                send(edge.at[1, i], came.at[0, i], edge_send.at[1], edge_sem.at[0, i], high_seat, m)

        def add_edge(side, i, row):
            @pl.when(has_high if side else has_low)
            def _():
                wait_for(came.at[side, i], edge_sem.at[side, i])
                for j in range(2):
                    total[side, i, j] = (scaled(1 + side, row, j) + came[side, i, j].astype(F32)).astype(BF16)

            @pl.when(jnp.logical_not(has_high if side else has_low))
            def _():
                for j in range(2):
                    total[side, i, j] = scaled(1 + side, row, j).astype(BF16)

        def finish(i):
            row = row_of(i)
            for side in (1, 0):
                add_edge(side, i, row)

                @pl.when(i == 0)
                def _():
                    send(
                        total.at[side, i], passed.at[side],
                        part_send.at[side], part_sem.at[side], other_seat, m,
                    )

                @pl.when(i == 1)
                def _():
                    wait_for(passed.at[side], part_sem.at[side])
                    total[side, i] = (total[side, i].astype(F32) + passed[side].astype(F32)).astype(BF16)

                @pl.when(i > 0)
                def _():
                    seat, m0 = seat_of(side, row - 1)

                    def send_tile(j, carry):
                        for n, ref in ((0, gk_out), (1, gv_out)):
                            send(
                                total.at[side, i, n, j // 2, tile_rows(lax.rem(j, 2)), :], ref.at[:, columns],
                                total_send, token_sem.at[2 + n], seat, m0 + j,
                            )
                        return carry

                    lax.fori_loop(0, TW, send_tile, 0)

        def step(i, carry):
            r = jnp.where(part == 0, 3 - i, i)

            def one(layer, carry):
                strip(layer, r)
                send_strip(layer, r)
                return carry

            lax.fori_loop(0, 2, one, 0)
            send_edge(i)

            @pl.when(i > 0)
            def _():
                finish(i - 1)

            return carry

        lax.fori_loop(0, 4, step, 0)
        send_edge(4)

        def last(i, carry):
            finish(i)
            return carry

        lax.fori_loop(3, 5, last, 0)

        wait_for(out, out_send)
        wait_for(total.at[:, pl.ds(1, 4)], total_send)
        for side in range(2):
            wait_for(pool.at[0, 0], zsend.at[side])
            wait_for(total.at[side, 0], part_send.at[side])

            @pl.when(has_high if side else has_low)
            def _():
                wait_for(pool.at[0, pl.ds(0, 5)], xsend.at[side])
                wait_for(edge.at[side], edge_send.at[side])

    pl.when(active)(work)

    for i, ref in enumerate((k_ref, v_ref, q_ref, g_ref)):
        wait_for(ref, send_sem.at[i])
    for i in range(WAVES):
        wait_for(flag_mine, flag_send.at[i])
    for i, ref in enumerate((att_out, gq_out, gk_out, gv_out)):
        wait_for(ref, token_sem.at[i])


def on_device(queries, keys, values, out_grad, window_lists, valid_counts):
    any_space = pl.BlockSpec(memory_space=pl.ANY)
    dma = pltpu.SemaphoreType.DMA
    row = (2, 2, 2 * TILE, HEAD_DIM)
    return pl.pallas_call(
        kernel,
        out_shape=(jax.ShapeDtypeStruct((TILE, D), BF16),) * 4,
        in_specs=[any_space] * 4
        + [pl.BlockSpec(memory_space=pltpu.VMEM), pl.BlockSpec(memory_space=pltpu.SMEM)],
        out_specs=(any_space,) * 4,
        scratch_shapes=[
            pltpu.VMEM((4, 6) + row, BF16),
            pltpu.VMEM((2, 4, 2, TW * TILE, HEAD_DIM), BF16),
            pltpu.VMEM((2, 4, 2, TW * TILE, HEAD_DIM), BF16),
            pltpu.VMEM((4, 6) + row, F32),
            pltpu.VMEM((2, 5) + row, BF16),
            pltpu.VMEM((2, 5) + row, BF16),
            pltpu.VMEM((2,) + row, BF16),
            pltpu.VMEM((2, 5) + row, BF16),
            pltpu.VMEM((8, 128), F32),
            pltpu.VMEM((2, 2, 8, 128), F32),
            pltpu.VMEM((2, 128, KEYS), BF16),
            pltpu.VMEM((4, 6, 2, 128), F32),
            pltpu.VMEM((2, 4, 2, 4, KEYS), F32),
            dma((4,)), dma((2, 4)), dma((2, 4)), dma((WAVES,)), dma((2, 2)),
            dma((2,)), dma((2, 6)), dma((2,)), dma((2,)),
            dma, dma((4,)), dma((2,)), dma((2, 5)), dma((2,)), dma((2,)), dma,
        ],
        compiler_params=pltpu.CompilerParams(
            collective_id=0, has_side_effects=True, vmem_limit_bytes=56 * 1024 * 1024
        ),
        cost_estimate=pl.CostEstimate(flops=5_400_000_000, bytes_accessed=6_000_000, transcendentals=3_600_000),
        name="window_attention",
    )(queries, keys, values, out_grad, window_lists, valid_counts)


def solution(mesh):
    rows = P(("seq", "mp"), None)
    return jax.shard_map(
        on_device,
        mesh=mesh,
        in_specs=(rows, rows, rows, rows, P("seq", None), P()),
        out_specs=(rows, rows, rows, rows),
        check_vma=False,
    )
```

time: 915 us -> 120 us (0.13)
  the two profiles are of different devices: /device:TPU:68 before, /device:TPU:1 now
where the time goes in v2:
time: 120 us
  Pallas kernels  114 us (95%)
  local copies, waits for them, and re-layouts  4.84 us (4%)
    pallas_call x1, Pallas kernels, on_device(): pl.pallas_call(kernel, out_shape=(jax.ShapeDtypeStruct((TILE, D), BF16),)...  114 us
    unnamed x10, local copies, waits for them, and re-layouts  4.84 us

profile of v2, /device:TPU:1, one launch (start us, length us, event | category | flops | bytes accessed | tf_op | source)
XLA Modules:
  0.0 120.0 jit_solution(14526853005865581762)
XLA Ops:
  0.6 114.5 %window_attention.1 = (bf16[64,3072]{1,0:T(8,128)(2,1)}, bf16[64,3072]{1,0:T(8,128)(2,1)}, bf16[64,3072]{1,0:T(8,128)(2,1)}, bf16[64,3072]{1,0:T(8,128)(2,1)}) custom-call(bf16[64,3072]{1,0:T(8,128)(2,1)} %q_ref.1, bf16[64,3072]{1,0:T(8,128)(2,1)} %k_ref.1, bf16[64,3072]{1,0:T(8,128)(2,1)} %v_ref.1, bf16[64,3072]{1,0:T(8,128)(2,1)} %g_ref.1, ...), custom_call_target="tpu_custom_call" | custom-call | flops 5400000000 | bytes 6000000 | tf_op jit(solution)/shard_map/window_attention/pallas_call | solution.py:456
  115.1 0.0 copy-start.2
  115.1 1.8 %copy.14 = bf16[64,3072]{1,0:T(8,128)(2,1)} copy(bf16[64,3072]{1,0:T(8,128)(2,1)} %get-tuple-element.8) | data formatting | bytes 786432
  117.0 0.0 copy-done.2
  117.0 0.0 copy-start.1
  117.0 0.7 copy.15
  117.7 0.4 copy-done.1
  118.1 0.0 copy-start
  118.1 0.7 copy.16
  118.8 0.4 copy-done
  119.2 0.7 copy.17
Async XLA Ops:
  115.1 1.8 %copy-start.2 = (bf16[64,3072]{1,0:T(8,128)(2,1)S(1)}, bf16[64,3072]{1,0:T(8,128)(2,1)}, u32[]{:S(2)}) copy-start(bf16[64,3072]{1,0:T(8,128)(2,1)} %get-tuple-element.9) | copy-start | bytes 1179652
  117.0 1.1 copy-start.1
  118.1 1.1 copy-start

commit v3 on v2

--- a/solution.py
+++ b/solution.py
@@ -141,8 +141,8 @@
 
     my_rows = tile_rows(lax.rem(w, 2))
 
-    def send_wave(number, carry):
-        def send_kv(j, carry):
+    def send_kv(number):
+        def one(j, carry):
             wm = lax.rem(j + m + z, NM)
             seat = x * NZ + worker_z(own, wm, number)
             columns = head_columns(3 * wm + number)
@@ -154,7 +154,16 @@
                 )
             return carry
 
-        def send_qg(j, carry):
+        lax.fori_loop(0, NM, one, 0)
+
+    def send_qg(number):
+        send(
+            flag_mine, flag_all.at[zh, lax.rem(zl, 2)],
+            flag_send.at[number], flag_sem.at[zh, lax.rem(zl, 2)],
+            x * NZ + worker_z(own, m, number), m,
+        )
+
+        def one(j, carry):
             wm = lax.rem(j + m + z, NM)
             seat = x * NZ + worker_z(own, wm, number)
             columns = head_columns(3 * wm + number)
@@ -166,19 +175,51 @@
                 )
             return carry
 
-        lax.fori_loop(0, NM, send_kv, 0)
-        send(
-            flag_mine, flag_all.at[zh, lax.rem(zl, 2)],
-            flag_send.at[number], flag_sem.at[zh, lax.rem(zl, 2)],
-            x * NZ + worker_z(own, m, number), m,
-        )
-        lax.fori_loop(0, NM, send_qg, 0)
-        return carry
-
-    lax.fori_loop(0, WAVES, send_wave, 0)
+        lax.fori_loop(0, NM, one, 0)
 
     def row_of(i):
         return jnp.where(part == 0, 5 - i, i)
+
+    def forward(i, carry):
+        row = row_of(i)
+        for side in range(2):
+            @pl.when(i > 0)
+            def _():
+                wait_for(pool.at[1 + side, row], kv_sem.at[side, jnp.maximum(row, 1) - 1])
+
+            @pl.when(i == 0)
+            def _():
+                wait_for(pool.at[1 + side, row], zsem.at[side])
+
+            @pl.when(i == 1)
+            def _():
+                send(
+                    pool.at[1 + side, row], pool.at[1 + side, jnp.where(part == 0, 0, 5)],
+                    zsend.at[side], zsem.at[side], other_seat, m,
+                )
+
+        @pl.when(has_low)
+        def _():
+            send(pool.at[1, row], pool.at[3, row], xsend.at[0], xsem.at[1, row], low_seat, m)
+
+        @pl.when(has_high)
+        def _():
+            send(pool.at[2, row], pool.at[0, row], xsend.at[1], xsem.at[0, row], high_seat, m)
+
+        return carry
+
+    def send_wave(number, carry):
+        send_kv(number)
+        send_qg(number)
+
+        @pl.when(jnp.logical_and(active, wave == number))
+        def _():
+            lax.fori_loop(1, 5, forward, 0)
+            forward(0, 0)
+
+        return carry
+
+    lax.fori_loop(0, WAVES, send_wave, 0)
 
     def work():
         acc[...] = jnp.zeros_like(acc)
@@ -204,37 +245,6 @@
         for pair in range(2):
             wanted = key // 128 * 4 + pair * 2 + lax.rem(key, 128) // TILE
             places[pair] = jnp.where(wanted == flag, 1.0, 0.0).astype(BF16)
-
-        def forward(i, carry):
-            row = row_of(i)
-            for side in range(2):
-                @pl.when(i > 0)
-                def _():
-                    wait_for(pool.at[1 + side, row], kv_sem.at[side, jnp.maximum(row, 1) - 1])
-
-                @pl.when(i == 0)
-                def _():
-                    wait_for(pool.at[1 + side, row], zsem.at[side])
-
-                @pl.when(i == 1)
-                def _():
-                    send(
-                        pool.at[1 + side, row], pool.at[1 + side, jnp.where(part == 0, 0, 5)],
-                        zsend.at[side], zsem.at[side], other_seat, m,
-                    )
-
-            @pl.when(has_low)
-            def _():
-                send(pool.at[1, row], pool.at[3, row], xsend.at[0], xsem.at[1, row], low_seat, m)
-
-            @pl.when(has_high)
-            def _():
-                send(pool.at[2, row], pool.at[0, row], xsend.at[1], xsem.at[0, row], high_seat, m)
-
-            return carry
-
-        lax.fori_loop(1, 5, forward, 0)
-        forward(0, 0)
 
         def make_bias(layer, carry):
             for a in range(2):

time: 120 us -> 116 us (0.967)
  Pallas kernels: 114 us -> 109 us
    pallas_call x1, Pallas kernels: 114 us -> 109 us  [on_device(): pl.pallas_call(kernel, out_shape=(jax.ShapeDtypeStruct((TILE, D), BF16),)...]
where the time goes in v3:
time: 116 us; the launch traced here: 115 us
  Pallas kernels  109 us (94%)
  local copies, waits for them, and re-layouts  4.84 us (4%)
    pallas_call x1, Pallas kernels, on_device(): pl.pallas_call(kernel, out_shape=(jax.ShapeDtypeStruct((TILE, D), BF16),)...  109 us
    unnamed x10, local copies, waits for them, and re-layouts  4.84 us

profile of v3, /device:TPU:1, one launch (start us, length us, event | category | flops | bytes accessed | tf_op | source)
XLA Modules:
  0.0 115.0 jit_solution(8517976943349324553)
XLA Ops:
  0.6 109.5 %window_attention.1 = (bf16[64,3072]{1,0:T(8,128)(2,1)}, bf16[64,3072]{1,0:T(8,128)(2,1)}, bf16[64,3072]{1,0:T(8,128)(2,1)}, bf16[64,3072]{1,0:T(8,128)(2,1)}) custom-call(bf16[64,3072]{1,0:T(8,128)(2,1)} %q_ref.1, bf16[64,3072]{1,0:T(8,128)(2,1)} %k_ref.1, bf16[64,3072]{1,0:T(8,128)(2,1)} %v_ref.1, bf16[64,3072]{1,0:T(8,128)(2,1)} %g_ref.1, ...), custom_call_target="tpu_custom_call" | custom-call | flops 5400000000 | bytes 6000000 | tf_op jit(solution)/shard_map/window_attention/pallas_call | solution.py:466
  110.1 0.0 copy-start.2
  110.1 1.8 %copy.14 = bf16[64,3072]{1,0:T(8,128)(2,1)} copy(bf16[64,3072]{1,0:T(8,128)(2,1)} %get-tuple-element.8) | data formatting | bytes 786432
  112.0 0.0 copy-done.2
  112.0 0.0 copy-start.1
  112.0 0.7 copy.15
  112.7 0.4 copy-done.1
  113.1 0.0 copy-start
  113.1 0.7 copy.16
  113.8 0.4 copy-done
  114.2 0.7 copy.17
Async XLA Ops:
  110.1 1.8 %copy-start.2 = (bf16[64,3072]{1,0:T(8,128)(2,1)S(1)}, bf16[64,3072]{1,0:T(8,128)(2,1)}, u32[]{:S(2)}) copy-start(bf16[64,3072]{1,0:T(8,128)(2,1)} %get-tuple-element.9) | copy-start | bytes 1179652
  112.0 1.1 copy-start.1
  113.1 1.1 copy-start

commit v4 on v3

--- a/solution.py
+++ b/solution.py
@@ -141,7 +141,7 @@
 
     my_rows = tile_rows(lax.rem(w, 2))
 
-    def send_kv(number):
+    def send_kv(number, start, stop):
         def one(j, carry):
             wm = lax.rem(j + m + z, NM)
             seat = x * NZ + worker_z(own, wm, number)
@@ -154,15 +154,16 @@
                 )
             return carry
 
-        lax.fori_loop(0, NM, one, 0)
-
-    def send_qg(number):
+        lax.fori_loop(start, stop, one, 0)
+
+    def send_flags(number):
         send(
             flag_mine, flag_all.at[zh, lax.rem(zl, 2)],
             flag_send.at[number], flag_sem.at[zh, lax.rem(zl, 2)],
             x * NZ + worker_z(own, m, number), m,
         )
 
+    def send_qg(number, start, stop):
         def one(j, carry):
             wm = lax.rem(j + m + z, NM)
             seat = x * NZ + worker_z(own, wm, number)
@@ -175,7 +176,7 @@
                 )
             return carry
 
-        lax.fori_loop(0, NM, one, 0)
+        lax.fori_loop(start, stop, one, 0)
 
     def row_of(i):
         return jnp.where(part == 0, 5 - i, i)
@@ -208,18 +209,34 @@
 
         return carry
 
-    def send_wave(number, carry):
-        send_kv(number)
-        send_qg(number)
-
+    def forward_own(number):
         @pl.when(jnp.logical_and(active, wave == number))
         def _():
             lax.fori_loop(1, 5, forward, 0)
+
+    def forward_other(number):
+        @pl.when(jnp.logical_and(active, wave == number))
+        def _():
             forward(0, 0)
 
-        return carry
-
-    lax.fori_loop(0, WAVES, send_wave, 0)
+    send_flags(0)
+    send_kv(0, 0, 8)
+    send_flags(1)
+    send_kv(1, 0, 8)
+    send_flags(2)
+    send_kv(2, 0, 8)
+    send_qg(0, 0, 4)
+    forward_own(0)
+    send_qg(0, 4, 8)
+    forward_own(1)
+    send_qg(1, 0, 4)
+    forward_other(0)
+    send_qg(1, 4, 8)
+    forward_own(2)
+    send_qg(2, 0, 4)
+    forward_other(1)
+    send_qg(2, 4, 8)
+    forward_other(2)
 
     def work():
         acc[...] = jnp.zeros_like(acc)

time: 116 us -> 111 us (0.957)
  Pallas kernels: 109 us -> 105 us
    pallas_call x1, Pallas kernels: 109 us -> 105 us  [on_device(): pl.pallas_call(kernel, out_shape=(jax.ShapeDtypeStruct((TILE, D), BF16),)...]
where the time goes in v4:
time: 111 us; the launch traced here: 110 us
  Pallas kernels  105 us (95%)
  local copies, waits for them, and re-layouts  4.84 us (4%)
    pallas_call x1, Pallas kernels, on_device(): pl.pallas_call(kernel, out_shape=(jax.ShapeDtypeStruct((TILE, D), BF16),)...  105 us
    unnamed x10, local copies, waits for them, and re-layouts  4.84 us

profile of v4, /device:TPU:1, one launch (start us, length us, event | category | flops | bytes accessed | tf_op | source)
XLA Modules:
  0.0 110.4 jit_solution(2718417029816708506)
XLA Ops:
  0.6 104.9 %window_attention.1 = (bf16[64,3072]{1,0:T(8,128)(2,1)}, bf16[64,3072]{1,0:T(8,128)(2,1)}, bf16[64,3072]{1,0:T(8,128)(2,1)}, bf16[64,3072]{1,0:T(8,128)(2,1)}) custom-call(bf16[64,3072]{1,0:T(8,128)(2,1)} %q_ref.1, bf16[64,3072]{1,0:T(8,128)(2,1)} %k_ref.1, bf16[64,3072]{1,0:T(8,128)(2,1)} %v_ref.1, bf16[64,3072]{1,0:T(8,128)(2,1)} %g_ref.1, ...), custom_call_target="tpu_custom_call" | custom-call | flops 5400000000 | bytes 6000000 | tf_op jit(solution)/shard_map/window_attention/pallas_call | solution.py:483
  105.5 0.0 copy-start.2
  105.6 1.8 %copy.14 = bf16[64,3072]{1,0:T(8,128)(2,1)} copy(bf16[64,3072]{1,0:T(8,128)(2,1)} %get-tuple-element.8) | data formatting | bytes 786432
  107.4 0.0 copy-done.2
  107.4 0.0 copy-start.1
  107.4 0.7 copy.15
  108.1 0.4 copy-done.1
  108.5 0.0 copy-start
  108.5 0.7 copy.16
  109.3 0.4 copy-done
  109.6 0.7 copy.17
Async XLA Ops:
  105.5 1.8 %copy-start.2 = (bf16[64,3072]{1,0:T(8,128)(2,1)S(1)}, bf16[64,3072]{1,0:T(8,128)(2,1)}, u32[]{:S(2)}) copy-start(bf16[64,3072]{1,0:T(8,128)(2,1)} %get-tuple-element.9) | copy-start | bytes 1179652
  107.4 1.1 %copy-start.1 = (bf16[64,3072]{1,0:T(8,128)(2,1)S(1)}, bf16[64,3072]{1,0:T(8,128)(2,1)}, u32[]{:S(2)}) copy-start(bf16[64,3072]{1,0:T(8,128)(2,1)} %get-tuple-element.10) | copy-start | bytes 1179652
  108.5 1.1 %copy-start = (bf16[64,3072]{1,0:T(8,128)(2,1)S(1)}, bf16[64,3072]{1,0:T(8,128)(2,1)}, u32[]{:S(2)}) copy-start(bf16[64,3072]{1,0:T(8,128)(2,1)} %get-tuple-element.11) | copy-start | bytes 1179652

commit v5 on v4

--- a/solution.py
+++ b/solution.py
@@ -105,7 +105,7 @@
 
 def kernel(
     q_ref, k_ref, v_ref, g_ref, list_ref, count_ref,
-    att_out, gq_out, gk_out, gv_out,
+    tokens,
     pool, qg, out, acc, edge, came, passed, total, flag_mine, flag_all, places, valid, bias,
     send_sem, kv_sem, qg_sem, flag_send, flag_sem, xsend, xsem, zsend, zsem,
     out_send, token_sem, edge_send, edge_sem, part_send, part_sem, total_send,
@@ -224,19 +224,19 @@
     send_flags(1)
     send_kv(1, 0, 8)
     send_flags(2)
-    send_kv(2, 0, 8)
+    send_kv(2, 0, 4)
+    forward_own(0)
+    send_kv(2, 4, 8)
     send_qg(0, 0, 4)
-    forward_own(0)
+    forward_own(1)
     send_qg(0, 4, 8)
-    forward_own(1)
+    forward_other(0)
+    forward_own(2)
     send_qg(1, 0, 4)
-    forward_other(0)
+    forward_other(1)
     send_qg(1, 4, 8)
-    forward_own(2)
-    send_qg(2, 0, 4)
-    forward_other(1)
-    send_qg(2, 4, 8)
     forward_other(2)
+    send_qg(2, 0, 8)
 
     def work():
         acc[...] = jnp.zeros_like(acc)
@@ -359,11 +359,10 @@
             seat, m0 = seat_of(layer, r)
 
             def send_tile(j, carry):
-                for i, ref in ((0, att_out), (1, gq_out)):
-                    send(
-                        out.at[layer, r, i, tile_rows(j), :], ref.at[:, columns],
-                        out_send, token_sem.at[i], seat, m0 + j,
-                    )
+                send(
+                    out.at[layer, r, :, tile_rows(j), :], tokens.at[pl.ds(0, 2), :, columns],
+                    out_send, token_sem.at[0], seat, m0 + j,
+                )
                 return carry
 
             lax.fori_loop(0, TW, send_tile, 0)
@@ -371,63 +370,58 @@
         def scaled(layer, row, i):
             return acc[layer, row, i] * (SCALE if i == 0 else 1.0)
 
-        def send_edge(i):
+        def has(side):
+            return jnp.where(side == 0, x, NX - 1 - x) > 0
+
+        def send_edge(i, side):
+            @pl.when(has(side))
+            def _():
+                for j in range(2):
+                    edge[side, i, j] = scaled(3 * side, row_of(i), j).astype(BF16)
+                send(
+                    edge.at[side, i], came.at[1 - side, i], edge_send.at[side], edge_sem.at[1 - side, i],
+                    jnp.where(side == 0, low_seat, high_seat), m,
+                )
+
+        def finish(i, side):
             row = row_of(i)
 
-            @pl.when(has_low)
-            def _():
-                for j in range(2):
-                    edge[0, i, j] = scaled(0, row, j).astype(BF16)
-                send(edge.at[0, i], came.at[1, i], edge_send.at[0], edge_sem.at[1, i], low_seat, m)
-
-            @pl.when(has_high)
-            def _():
-                for j in range(2):
-                    edge[1, i, j] = scaled(3, row, j).astype(BF16)
-                send(edge.at[1, i], came.at[0, i], edge_send.at[1], edge_sem.at[0, i], high_seat, m)
-
-        def add_edge(side, i, row):
-            @pl.when(has_high if side else has_low)
+            @pl.when(has(side))
             def _():
                 wait_for(came.at[side, i], edge_sem.at[side, i])
                 for j in range(2):
                     total[side, i, j] = (scaled(1 + side, row, j) + came[side, i, j].astype(F32)).astype(BF16)
 
-            @pl.when(jnp.logical_not(has_high if side else has_low))
+            @pl.when(jnp.logical_not(has(side)))
             def _():
                 for j in range(2):
                     total[side, i, j] = scaled(1 + side, row, j).astype(BF16)
 
-        def finish(i):
-            row = row_of(i)
-            for side in (1, 0):
-                add_edge(side, i, row)
-
-                @pl.when(i == 0)
-                def _():
+            @pl.when(i == 0)
+            def _():
+                send(
+                    total.at[side, i], passed.at[side],
+                    part_send.at[side], part_sem.at[side], other_seat, m,
+                )
+
+            @pl.when(i == 1)
+            def _():
+                wait_for(passed.at[side], part_sem.at[side])
+                total[side, i] = (total[side, i].astype(F32) + passed[side].astype(F32)).astype(BF16)
+
+            @pl.when(i > 0)
+            def _():
+                seat, m0 = seat_of(side, row - 1)
+
+                def send_tile(j, carry):
                     send(
-                        total.at[side, i], passed.at[side],
-                        part_send.at[side], part_sem.at[side], other_seat, m,
+                        total.at[side, i, :, j // 2, tile_rows(lax.rem(j, 2)), :],
+                        tokens.at[pl.ds(2, 2), :, columns],
+                        total_send, token_sem.at[1], seat, m0 + j,
                     )
-
-                @pl.when(i == 1)
-                def _():
-                    wait_for(passed.at[side], part_sem.at[side])
-                    total[side, i] = (total[side, i].astype(F32) + passed[side].astype(F32)).astype(BF16)
-
-                @pl.when(i > 0)
-                def _():
-                    seat, m0 = seat_of(side, row - 1)
-
-                    def send_tile(j, carry):
-                        for n, ref in ((0, gk_out), (1, gv_out)):
-                            send(
-                                total.at[side, i, n, j // 2, tile_rows(lax.rem(j, 2)), :], ref.at[:, columns],
-                                total_send, token_sem.at[2 + n], seat, m0 + j,
-                            )
-                        return carry
-
-                    lax.fori_loop(0, TW, send_tile, 0)
+                    return carry
+
+                lax.fori_loop(0, TW, send_tile, 0)
 
         def step(i, carry):
             r = jnp.where(part == 0, 3 - i, i)
@@ -435,25 +429,28 @@
             def one(layer, carry):
                 strip(layer, r)
                 send_strip(layer, r)
+                send_edge(i, layer)
+
+                @pl.when(i == 3)
+                def _():
+                    send_edge(4, layer)
+
+                @pl.when(jnp.logical_and(i > 0, layer == 0))
+                def _():
+                    finish(i - 1, 1)
+                    finish(i - 1, 0)
+
                 return carry
 
-            lax.fori_loop(0, 2, one, 0)
-            send_edge(i)
-
-            @pl.when(i > 0)
-            def _():
-                finish(i - 1)
-
+            return lax.fori_loop(0, 2, one, carry)
+
+        lax.fori_loop(0, 4, step, 0)
+
+        def last(n, carry):
+            finish(3 + lax.rem(n, 2), 1 - n // 2)
             return carry
 
-        lax.fori_loop(0, 4, step, 0)
-        send_edge(4)
-
-        def last(i, carry):
-            finish(i)
-            return carry
-
-        lax.fori_loop(3, 5, last, 0)
+        lax.fori_loop(0, 4, last, 0)
 
         wait_for(out, out_send)
         wait_for(total.at[:, pl.ds(1, 4)], total_send)
@@ -472,20 +469,25 @@
         wait_for(ref, send_sem.at[i])
     for i in range(WAVES):
         wait_for(flag_mine, flag_send.at[i])
-    for i, ref in enumerate((att_out, gq_out, gk_out, gv_out)):
-        wait_for(ref, token_sem.at[i])
+    for i in range(2):
+        wait_for(tokens.at[pl.ds(2 * i, 2)], token_sem.at[i])
+
+
+def relay_kernel(tokens, *outs):
+    for i, ref in enumerate(outs):
+        ref[...] = tokens[i]
 
 
 def on_device(queries, keys, values, out_grad, window_lists, valid_counts):
     any_space = pl.BlockSpec(memory_space=pl.ANY)
     dma = pltpu.SemaphoreType.DMA
     row = (2, 2, 2 * TILE, HEAD_DIM)
-    return pl.pallas_call(
+    tokens = pl.pallas_call(
         kernel,
-        out_shape=(jax.ShapeDtypeStruct((TILE, D), BF16),) * 4,
+        out_shape=jax.ShapeDtypeStruct((4, TILE, D), BF16),
         in_specs=[any_space] * 4
         + [pl.BlockSpec(memory_space=pltpu.VMEM), pl.BlockSpec(memory_space=pltpu.SMEM)],
-        out_specs=(any_space,) * 4,
+        out_specs=any_space,
         scratch_shapes=[
             pltpu.VMEM((4, 6) + row, BF16),
             pltpu.VMEM((2, 4, 2, TW * TILE, HEAD_DIM), BF16),
@@ -502,7 +504,7 @@
             pltpu.VMEM((2, 4, 2, 4, KEYS), F32),
             dma((4,)), dma((2, 4)), dma((2, 4)), dma((WAVES,)), dma((2, 2)),
             dma((2,)), dma((2, 6)), dma((2,)), dma((2,)),
-            dma, dma((4,)), dma((2,)), dma((2, 5)), dma((2,)), dma((2,)), dma,
+            dma, dma((2,)), dma((2,)), dma((2, 5)), dma((2,)), dma((2,)), dma,
         ],
         compiler_params=pltpu.CompilerParams(
             collective_id=0, has_side_effects=True, vmem_limit_bytes=56 * 1024 * 1024
@@ -510,6 +512,16 @@
         cost_estimate=pl.CostEstimate(flops=5_400_000_000, bytes_accessed=6_000_000, transcendentals=3_600_000),
         name="window_attention",
     )(queries, keys, values, out_grad, window_lists, valid_counts)
+
+    block = pl.BlockSpec((16, D), lambda i: (i, 0))
+    return pl.pallas_call(
+        relay_kernel,
+        grid=(TILE // 16,),
+        out_shape=(jax.ShapeDtypeStruct((TILE, D), BF16),) * 4,
+        in_specs=[pl.BlockSpec((4, 16, D), lambda i: (0, i, 0))],
+        out_specs=(block,) * 4,
+        name="relay",
+    )(tokens)
 
 
 def solution(mesh):

time: 111 us -> 106 us (0.955)
  local copies, waits for them, and re-layouts: 4.84 us -> 0 us
    unnamed x10 -> x0, local copies, waits for them, and re-layouts: 4.84 us -> none
    pallas_call x1 -> x2, Pallas kernels: 105 us -> 105 us  [the longest x1 102 us: on_device(): pl.pallas_call(kernel, out_shape=jax.ShapeDtypeStruct((4, TILE, D), BF16)...]
where the time goes in v5:
time: 106 us
  Pallas kernels  105 us (99%)
    pallas_call x1, Pallas kernels, on_device(): pl.pallas_call(kernel, out_shape=jax.ShapeDtypeStruct((4, TILE, D), BF16)...  102 us
    pallas_call x1, Pallas kernels, on_device(): pl.pallas_call(relay_kernel, grid=(TILE // 16,), out_shape=(jax.ShapeDtyp...  3.57 us

profile of v5, /device:TPU:1, one launch (start us, length us, event | category | flops | bytes accessed | tf_op | source)
XLA Modules:
  0.0 106.1 jit_solution(11844208994739731739)
XLA Ops:
  0.6 101.9 %window_attention.1.tokens = bf16[4,64,3072]{2,1,0:T(8,128)(2,1)} custom-call(bf16[64,3072]{1,0:T(8,128)(2,1)} %q_ref.1, bf16[64,3072]{1,0:T(8,128)(2,1)} %k_ref.1, bf16[64,3072]{1,0:T(8,128)(2,1)} %v_ref.1, bf16[64,3072]{1,0:T(8,128)(2,1)} %g_ref.1, s32[8,27]{1,0:T(8,128)} %list_ref.1, s32[256]{0:T(256)} %count_ref.1), custom_call_target="tpu_custom_call" | custom-call | flops 5400000000 | bytes 6000000 | tf_op jit(solution)/shard_map/window_attention/pallas_call | solution.py:485
  102.5 3.6 %relay.1 = (bf16[64,3072]{1,0:T(8,128)(2,1)}, bf16[64,3072]{1,0:T(8,128)(2,1)}, bf16[64,3072]{1,0:T(8,128)(2,1)}, bf16[64,3072]{1,0:T(8,128)(2,1)}) custom-call(bf16[4,64,3072]{2,1,0:T(8,128)(2,1)} %window_attention.1.tokens), custom_call_target="tpu_custom_call" | custom-call | tf_op jit(solution)/shard_map/relay/pallas_call | solution.py:517

commit v6 on v5

--- a/solution.py
+++ b/solution.py
@@ -53,31 +53,32 @@
     return part, wave, jnp.logical_or(same_u, same_v)
 
 
-def greet_plane(x, z, m):
+def greet(x, z, m, part, wave, active):
     barrier = pltpu.get_barrier_semaphore()
 
-    def greet(i, carry):
-        zz = i // NM
-        mm = lax.rem(i, NM)
-
-        @pl.when(jnp.logical_or(zz != z, mm != m))
+    def signal(seat, mm):
+        pl.semaphore_signal(barrier, inc=1, device_id=(seat, mm), device_id_type=MESH)
+
+    @pl.when(active)
+    def _():
+        def owner(d, carry):
+            zz = 2 * part + lax.rem(d // NM, 2) + 4 * (d // (2 * NM))
+            signal(x * NZ + zz, lax.rem(m + d, NM))
+            return carry
+
+        lax.fori_loop(0, 4 * NM, owner, 0)
+        signal(x * NZ + worker_z(1 - part, m, wave), m)
+
+        @pl.when(x > 0)
         def _():
-            pl.semaphore_signal(barrier, inc=1, device_id=(x * NZ + zz, mm), device_id_type=MESH)
-
-        return carry
-
-    lax.fori_loop(0, NZ * NM, greet, 0)
-
-    @pl.when(x > 0)
-    def _():
-        pl.semaphore_signal(barrier, inc=1, device_id=((x - 1) * NZ + z, m), device_id_type=MESH)
-
-    @pl.when(x < NX - 1)
-    def _():
-        pl.semaphore_signal(barrier, inc=1, device_id=((x + 1) * NZ + z, m), device_id_type=MESH)
-
-    peers = NZ * NM - 1 + jnp.where(x > 0, 1, 0) + jnp.where(x < NX - 1, 1, 0)
-    pl.semaphore_wait(barrier, peers)
+            signal((x - 1) * NZ + z, m)
+
+        @pl.when(x < NX - 1)
+        def _():
+            signal((x + 1) * NZ + z, m)
+
+    near = 1 + jnp.where(x > 0, 1, 0) + jnp.where(x < NX - 1, 1, 0)
+    pl.semaphore_wait(barrier, HEADS + jnp.where(active, near, 0))
 
 
 def wait_for(ref, sem):
@@ -137,7 +138,7 @@
         listed = jnp.where(list_ref[:, j : j + 1] == near, 1.0, listed)
     flag_mine[...] = listed
     pool[...] = jnp.zeros_like(pool)
-    greet_plane(x, z, m)
+    greet(x, z, m, part, wave, active)
 
     my_rows = tile_rows(lax.rem(w, 2))
 
@@ -473,9 +474,16 @@
         wait_for(tokens.at[pl.ds(2 * i, 2)], token_sem.at[i])
 
 
-def relay_kernel(tokens, *outs):
-    for i, ref in enumerate(outs):
-        ref[...] = tokens[i]
+def relay_kernel(tokens, a, b, c, d, held, load_sem, store_sem):
+    loads = [pltpu.make_async_copy(tokens.at[i], held.at[i], load_sem.at[i]) for i in range(4)]
+    stores = [pltpu.make_async_copy(held.at[i], ref, store_sem.at[i]) for i, ref in enumerate((a, b, c, d))]
+    for copy in loads:
+        copy.start()
+    for load, store in zip(loads, stores):
+        load.wait()
+        store.start()
+    for copy in stores:
+        copy.wait()
 
 
 def on_device(queries, keys, values, out_grad, window_lists, valid_counts):
@@ -513,13 +521,12 @@
         name="window_attention",
     )(queries, keys, values, out_grad, window_lists, valid_counts)
 
-    block = pl.BlockSpec((16, D), lambda i: (i, 0))
     return pl.pallas_call(
         relay_kernel,
-        grid=(TILE // 16,),
         out_shape=(jax.ShapeDtypeStruct((TILE, D), BF16),) * 4,
-        in_specs=[pl.BlockSpec((4, 16, D), lambda i: (0, i, 0))],
-        out_specs=(block,) * 4,
+        in_specs=[any_space],
+        out_specs=(any_space,) * 4,
+        scratch_shapes=[pltpu.VMEM((4, TILE, D), BF16), dma((4,)), dma((4,))],
         name="relay",
     )(tokens)
 

time: 106 us -> 104 us (0.981)
  Pallas kernels: 105 us -> 103 us
    pallas_call x1, Pallas kernels: 3.57 us -> 2.2 us  [on_device(): pl.pallas_call(relay_kernel, out_shape=(jax.ShapeDtypeStruct((TILE, D), B...]
where the time goes in v6:
time: 104 us
  Pallas kernels  103 us (99%)
    pallas_call x1, Pallas kernels, on_device(): pl.pallas_call(kernel, out_shape=jax.ShapeDtypeStruct((4, TILE, D), BF16)...  101 us
    pallas_call x1, Pallas kernels, on_device(): pl.pallas_call(relay_kernel, out_shape=(jax.ShapeDtypeStruct((TILE, D), B...  2.2 us

profile of v6, /device:TPU:1, one launch (start us, length us, event | category | flops | bytes accessed | tf_op | source)
XLA Modules:
  0.0 103.8 jit_solution(16264046822526192423)
XLA Ops:
  0.6 100.9 %window_attention.1.tokens = bf16[4,64,3072]{2,1,0:T(8,128)(2,1)} custom-call(bf16[64,3072]{1,0:T(8,128)(2,1)} %q_ref.1, bf16[64,3072]{1,0:T(8,128)(2,1)} %k_ref.1, bf16[64,3072]{1,0:T(8,128)(2,1)} %v_ref.1, bf16[64,3072]{1,0:T(8,128)(2,1)} %g_ref.1, s32[8,27]{1,0:T(8,128)} %list_ref.1, s32[256]{0:T(256)} %count_ref.1), custom_call_target="tpu_custom_call" | custom-call | flops 5400000000 | bytes 6000000 | tf_op jit(solution)/shard_map/window_attention/pallas_call | solution.py:493
  101.6 2.2 %relay.1 = (bf16[64,3072]{1,0:T(8,128)(2,1)}, bf16[64,3072]{1,0:T(8,128)(2,1)}, bf16[64,3072]{1,0:T(8,128)(2,1)}, bf16[64,3072]{1,0:T(8,128)(2,1)}) custom-call(bf16[4,64,3072]{2,1,0:T(8,128)(2,1)} %window_attention.1.tokens), custom_call_target="tpu_custom_call" | custom-call | tf_op jit(solution)/shard_map/relay/pallas_call | solution.py:524

commit v7 on v6

--- a/solution.py
+++ b/solution.py
@@ -53,7 +53,7 @@
     return part, wave, jnp.logical_or(same_u, same_v)
 
 
-def greet(x, z, m, part, wave, active):
+def greet(x, z, m, part, wave, active, two):
     barrier = pltpu.get_barrier_semaphore()
 
     def signal(seat, mm):
@@ -69,6 +69,18 @@
         lax.fori_loop(0, 4 * NM, owner, 0)
         signal(x * NZ + worker_z(1 - part, m, wave), m)
 
+        def border(d, carry):
+            zz = 2 - part + 4 * (z // 4)
+            mm = 4 * part + d
+
+            @pl.when(jnp.logical_or(zz != z, mm != m))
+            def _():
+                signal(x * NZ + zz, mm)
+
+            return carry
+
+        lax.fori_loop(0, TW, border, 0)
+
         @pl.when(x > 0)
         def _():
             signal((x - 1) * NZ + z, m)
@@ -78,7 +90,8 @@
             signal((x + 1) * NZ + z, m)
 
     near = 1 + jnp.where(x > 0, 1, 0) + jnp.where(x < NX - 1, 1, 0)
-    pl.semaphore_wait(barrier, HEADS + jnp.where(active, near, 0))
+    others = jnp.where(two, jnp.where(active, HEADS // 2 - 1, HEADS // 2), 0)
+    pl.semaphore_wait(barrier, HEADS + others + jnp.where(active, near, 0))
 
 
 def wait_for(ref, sem):
@@ -109,7 +122,7 @@
     tokens,
     pool, qg, out, acc, edge, came, passed, total, flag_mine, flag_all, places, valid, bias,
     send_sem, kv_sem, qg_sem, flag_send, flag_sem, xsend, xsem, zsend, zsem,
-    out_send, token_sem, edge_send, edge_sem, part_send, part_sem, total_send,
+    out_send, token_sem, edge_send, edge_sem, part_send, part_sem, total_send, border_send,
 ):
     x, z, m = place()
     zh = z // 4
@@ -124,7 +137,9 @@
     has_high = x < NX - 1
     low_seat = (x - 1) * NZ + z
     high_seat = (x + 1) * NZ + z
-    other_seat = x * NZ + worker_z(1 - part, m, wave)
+    other_z = worker_z(1 - part, m, wave)
+    other_seat = x * NZ + other_z
+    two = jnp.logical_or(h == 3, h == 4)
 
     spot = lax.broadcasted_iota(jnp.int32, (8, 128), 1)
     mine = lax.broadcasted_iota(jnp.int32, (8, 128), 0)
@@ -138,7 +153,7 @@
         listed = jnp.where(list_ref[:, j : j + 1] == near, 1.0, listed)
     flag_mine[...] = listed
     pool[...] = jnp.zeros_like(pool)
-    greet(x, z, m, part, wave, active)
+    greet(x, z, m, part, wave, active, two)
 
     my_rows = tile_rows(lax.rem(w, 2))
 
@@ -153,6 +168,22 @@
                     ref.at[:, columns], pool.at[1 + zh, 1 + row, i, w // 2, my_rows, :],
                     send_sem.at[i], kv_sem.at[zh, row], seat, wm,
                 )
+
+            oz = worker_z(1 - own, wm, number)
+            near = jnp.logical_and(two, oz // 4 == zh)
+            here = jnp.logical_and(oz == z, wm == m)
+            border = [pool.at[1 + zh, jnp.where(own == 0, 0, 5), i, w // 2, my_rows, :] for i in range(2)]
+
+            @pl.when(jnp.logical_and(near, jnp.logical_not(here)))
+            def _():
+                for i, ref in ((0, k_ref), (1, v_ref)):
+                    send(ref.at[:, columns], border[i], border_send.at[i], zsem.at[zh], x * NZ + oz, wm)
+
+            @pl.when(jnp.logical_and(near, here))
+            def _():
+                for i, ref in ((0, k_ref), (1, v_ref)):
+                    pltpu.make_async_copy(ref.at[:, columns], border[i], zsem.at[zh]).start()
+
             return carry
 
         lax.fori_loop(start, stop, one, 0)
@@ -193,7 +224,7 @@
             def _():
                 wait_for(pool.at[1 + side, row], zsem.at[side])
 
-            @pl.when(i == 1)
+            @pl.when(jnp.logical_and(i == 1, other_z // 4 != side))
             def _():
                 send(
                     pool.at[1 + side, row], pool.at[1 + side, jnp.where(part == 0, 0, 5)],
@@ -456,7 +487,11 @@
         wait_for(out, out_send)
         wait_for(total.at[:, pl.ds(1, 4)], total_send)
         for side in range(2):
-            wait_for(pool.at[0, 0], zsend.at[side])
+
+            @pl.when(other_z // 4 != side)
+            def _():
+                wait_for(pool.at[0, 0], zsend.at[side])
+
             wait_for(total.at[side, 0], part_send.at[side])
 
             @pl.when(has_high if side else has_low)
@@ -468,6 +503,15 @@
 
     for i, ref in enumerate((k_ref, v_ref, q_ref, g_ref)):
         wait_for(ref, send_sem.at[i])
+    for i, ref in enumerate((k_ref, v_ref)):
+        @pl.when(jnp.logical_and(two, active))
+        def _():
+            wait_for(ref.at[:, : (HEADS // 2 - 1) * HEAD_DIM], border_send.at[i])
+
+        @pl.when(jnp.logical_and(two, jnp.logical_not(active)))
+        def _():
+            wait_for(ref.at[:, : HEADS // 2 * HEAD_DIM], border_send.at[i])
+
     for i in range(WAVES):
         wait_for(flag_mine, flag_send.at[i])
     for i in range(2):
@@ -512,7 +556,7 @@
             pltpu.VMEM((2, 4, 2, 4, KEYS), F32),
             dma((4,)), dma((2, 4)), dma((2, 4)), dma((WAVES,)), dma((2, 2)),
             dma((2,)), dma((2, 6)), dma((2,)), dma((2,)),
-            dma, dma((2,)), dma((2,)), dma((2, 5)), dma((2,)), dma((2,)), dma,
+            dma, dma((2,)), dma((2,)), dma((2, 5)), dma((2,)), dma((2,)), dma, dma((2,)),
         ],
         compiler_params=pltpu.CompilerParams(
             collective_id=0, has_side_effects=True, vmem_limit_bytes=56 * 1024 * 1024

time: 104 us -> 102 us (0.981)
  Pallas kernels: 103 us -> 101 us
    pallas_call x1, Pallas kernels: 101 us -> 98.9 us  [on_device(): pl.pallas_call(kernel, out_shape=jax.ShapeDtypeStruct((4, TILE, D), BF16)...]
where the time goes in v7:
time: 102 us
  Pallas kernels  101 us (99%)
    pallas_call x1, Pallas kernels, on_device(): pl.pallas_call(kernel, out_shape=jax.ShapeDtypeStruct((4, TILE, D), BF16)...  98.9 us
    pallas_call x1, Pallas kernels, on_device(): pl.pallas_call(relay_kernel, out_shape=(jax.ShapeDtypeStruct((TILE, D), B...  2.2 us

profile of v7, /device:TPU:1, one launch (start us, length us, event | category | flops | bytes accessed | tf_op | source)
XLA Modules:
  0.0 101.7 jit_solution(659601448982344298)
XLA Ops:
  0.6 98.9 %window_attention.1.tokens = bf16[4,64,3072]{2,1,0:T(8,128)(2,1)} custom-call(bf16[64,3072]{1,0:T(8,128)(2,1)} %q_ref.1, bf16[64,3072]{1,0:T(8,128)(2,1)} %k_ref.1, bf16[64,3072]{1,0:T(8,128)(2,1)} %v_ref.1, bf16[64,3072]{1,0:T(8,128)(2,1)} %g_ref.1, s32[8,27]{1,0:T(8,128)} %list_ref.1, s32[256]{0:T(256)} %count_ref.1), custom_call_target="tpu_custom_call" | custom-call | flops 5400000000 | bytes 6000000 | tf_op jit(solution)/shard_map/window_attention/pallas_call | solution.py:537
  99.5 2.2 %relay.1 = (bf16[64,3072]{1,0:T(8,128)(2,1)}, bf16[64,3072]{1,0:T(8,128)(2,1)}, bf16[64,3072]{1,0:T(8,128)(2,1)}, bf16[64,3072]{1,0:T(8,128)(2,1)}) custom-call(bf16[4,64,3072]{2,1,0:T(8,128)(2,1)} %window_attention.1.tokens), custom_call_target="tpu_custom_call" | custom-call | tf_op jit(solution)/shard_map/relay/pallas_call | solution.py:568

commit v8 on v7

--- a/solution.py
+++ b/solution.py
@@ -36,7 +36,7 @@
 
 
 def worker_z(part, m, wave):
-    u = lax.rem(wave + m // 2, 2)
+    u = lax.rem(wave + 1, 2)
     v = lax.rem(m + wave // 2, 2)
     return jnp.where(part == 0, 3 - u + 4 * v, lax.rem(4 - 3 * u + 4 * v, NZ))
 
@@ -48,7 +48,7 @@
     u = jnp.where(part == 0, 3 - zq, zq)
     v = jnp.where(jnp.logical_and(part == 1, u == 0), 1 - zh, zh)
     same_v = v == lax.rem(m, 2)
-    same_u = u == lax.rem(m // 2, 2)
+    same_u = u == 1
     wave = jnp.where(same_u, jnp.where(same_v, 0, 2), 1)
     return part, wave, jnp.logical_or(same_u, same_v)
 
@@ -119,10 +119,10 @@
 
 def kernel(
     q_ref, k_ref, v_ref, g_ref, list_ref, count_ref,
-    tokens,
+    tokens, extra,
     pool, qg, out, acc, edge, came, passed, total, flag_mine, flag_all, places, valid, bias,
     send_sem, kv_sem, qg_sem, flag_send, flag_sem, xsend, xsem, zsend, zsem,
-    out_send, token_sem, edge_send, edge_sem, part_send, part_sem, total_send, border_send,
+    out_send, token_sem, edge_send, edge_sem, part_send, part_sem, total_send, border_send, near_send, extra_sem,
 ):
     x, z, m = place()
     zh = z // 4
@@ -385,7 +385,8 @@
         columns = head_columns(head)
 
         def seat_of(layer, row):
-            return x * NZ + layer * 4 + (4 * part + row) // 2, lax.rem(row, 2) * 4
+            there = 4 * part + row
+            return x * NZ + layer * 4 + there // 2, lax.rem(there, 2) * 4
 
         def send_strip(layer, r):
             seat, m0 = seat_of(layer, r)
@@ -429,14 +430,35 @@
                 for j in range(2):
                     total[side, i, j] = scaled(1 + side, row, j).astype(BF16)
 
-            @pl.when(i == 0)
+            @pl.when(jnp.logical_and(i == 0, side == z // 4))
+            def _():
+                seat, m0 = seat_of(side, row - 1)
+
+                def send_tile(j, carry):
+                    src = total.at[side, i, :, j // 2, tile_rows(lax.rem(j, 2)), :]
+                    dst = extra.at[:, :, columns]
+                    here = jnp.logical_and(two, m0 + j == m)
+
+                    @pl.when(here)
+                    def _():
+                        pltpu.make_async_copy(src, dst, extra_sem).start()
+
+                    @pl.when(jnp.logical_not(here))
+                    def _():
+                        send(src, dst, near_send, extra_sem, seat, m0 + j)
+
+                    return carry
+
+                lax.fori_loop(0, TW, send_tile, 0)
+
+            @pl.when(jnp.logical_and(i == 0, side != z // 4))
             def _():
                 send(
                     total.at[side, i], passed.at[side],
                     part_send.at[side], part_sem.at[side], other_seat, m,
                 )
 
-            @pl.when(i == 1)
+            @pl.when(jnp.logical_and(i == 1, side != other_z // 4))
             def _():
                 wait_for(passed.at[side], part_sem.at[side])
                 total[side, i] = (total[side, i].astype(F32) + passed[side].astype(F32)).astype(BF16)
@@ -484,6 +506,14 @@
 
         lax.fori_loop(0, 4, last, 0)
 
+        @pl.when(two)
+        def _():
+            wait_for(out.at[0, 0, :, pl.ds(0, 3 * TILE), :], near_send)
+
+        @pl.when(jnp.logical_not(two))
+        def _():
+            wait_for(out.at[0, 0], near_send)
+
         wait_for(out, out_send)
         wait_for(total.at[:, pl.ds(1, 4)], total_send)
         for side in range(2):
@@ -492,7 +522,11 @@
             def _():
                 wait_for(pool.at[0, 0], zsend.at[side])
 
-            wait_for(total.at[side, 0], part_send.at[side])
+
+            @pl.when(z // 4 != side)
+            def _():
+                wait_for(total.at[side, 0], part_send.at[side])
+
 
             @pl.when(has_high if side else has_low)
             def _():
@@ -517,15 +551,44 @@
     for i in range(2):
         wait_for(tokens.at[pl.ds(2 * i, 2)], token_sem.at[i])
 
-
-def relay_kernel(tokens, a, b, c, d, held, load_sem, store_sem):
+    @pl.when(two)
+    def _():
+        wait_for(extra.at[:, :, : HEADS // 2 * HEAD_DIM], extra_sem)
+
+
+def relay_kernel(tokens, extra, a, b, c, d, held, more, load_sem, more_sem, store_sem):
+    x, z, m = place()
+    h = 2 * lax.rem(z, 4) + m // 4
+    two = jnp.logical_or(h == 3, h == 4)
     loads = [pltpu.make_async_copy(tokens.at[i], held.at[i], load_sem.at[i]) for i in range(4)]
     stores = [pltpu.make_async_copy(held.at[i], ref, store_sem.at[i]) for i, ref in enumerate((a, b, c, d))]
-    for copy in loads:
+    extras = pltpu.make_async_copy(extra, more, more_sem)
+
+    @pl.when(two)
+    def _():
+        extras.start()
+
+    for copy in loads[2:] + loads[:2]:
         copy.start()
-    for load, store in zip(loads, stores):
-        load.wait()
-        store.start()
+    for i in (2, 3):
+        loads[i].wait()
+
+    @pl.when(two)
+    def _():
+        extras.wait()
+        for head in range(HEADS):
+            columns = slice(head * HEAD_DIM, (head + 1) * HEAD_DIM)
+
+            @pl.when(worker_z(jnp.where(h == 4, 0, 1), head // 3, head % 3) // 4 == z // 4)
+            def _():
+                both = held[2:, :, columns].astype(F32) + more[:, :, columns].astype(F32)
+                held[2:, :, columns] = both.astype(BF16)
+
+    for i in (2, 3):
+        stores[i].start()
+    for i in (0, 1):
+        loads[i].wait()
+        stores[i].start()
     for copy in stores:
         copy.wait()
 
@@ -534,12 +597,12 @@
     any_space = pl.BlockSpec(memory_space=pl.ANY)
     dma = pltpu.SemaphoreType.DMA
     row = (2, 2, 2 * TILE, HEAD_DIM)
-    tokens = pl.pallas_call(
+    tokens, extra = pl.pallas_call(
         kernel,
-        out_shape=jax.ShapeDtypeStruct((4, TILE, D), BF16),
+        out_shape=(jax.ShapeDtypeStruct((4, TILE, D), BF16), jax.ShapeDtypeStruct((2, TILE, D), BF16)),
         in_specs=[any_space] * 4
         + [pl.BlockSpec(memory_space=pltpu.VMEM), pl.BlockSpec(memory_space=pltpu.SMEM)],
-        out_specs=any_space,
+        out_specs=(any_space,) * 2,
         scratch_shapes=[
             pltpu.VMEM((4, 6) + row, BF16),
             pltpu.VMEM((2, 4, 2, TW * TILE, HEAD_DIM), BF16),
@@ -557,6 +620,7 @@
             dma((4,)), dma((2, 4)), dma((2, 4)), dma((WAVES,)), dma((2, 2)),
             dma((2,)), dma((2, 6)), dma((2,)), dma((2,)),
             dma, dma((2,)), dma((2,)), dma((2, 5)), dma((2,)), dma((2,)), dma, dma((2,)),
+            dma, dma,
         ],
         compiler_params=pltpu.CompilerParams(
             collective_id=0, has_side_effects=True, vmem_limit_bytes=56 * 1024 * 1024
@@ -568,11 +632,13 @@
     return pl.pallas_call(
         relay_kernel,
         out_shape=(jax.ShapeDtypeStruct((TILE, D), BF16),) * 4,
-        in_specs=[any_space],
+        in_specs=[any_space] * 2,
         out_specs=(any_space,) * 4,
-        scratch_shapes=[pltpu.VMEM((4, TILE, D), BF16), dma((4,)), dma((4,))],
+        scratch_shapes=[
+            pltpu.VMEM((4, TILE, D), BF16), pltpu.VMEM((2, TILE, D), BF16), dma((4,)), dma, dma((4,)),
+        ],
         name="relay",
-    )(tokens)
+    )(tokens, extra)
 
 
 def solution(mesh):

time: 102 us -> 98.5 us (0.966)
  Pallas kernels: 101 us -> 97.6 us
    pallas_call x1, Pallas kernels: 98.9 us -> 95.3 us  [on_device(): pl.pallas_call(kernel, out_shape=(jax.ShapeDtypeStruct((4, TILE, D), BF16...]
where the time goes in v8:
time: 98.5 us; the launch traced here: 98.3 us
  Pallas kernels  97.6 us (99%)
    pallas_call x1, Pallas kernels, on_device(): pl.pallas_call(kernel, out_shape=(jax.ShapeDtypeStruct((4, TILE, D), BF16...  95.3 us
    pallas_call x1, Pallas kernels, on_device(): pl.pallas_call(relay_kernel, out_shape=(jax.ShapeDtypeStruct((TILE, D), B...  2.33 us

profile of v8, /device:TPU:1, one launch (start us, length us, event | category | flops | bytes accessed | tf_op | source)
XLA Modules:
  0.0 98.3 jit_solution(14930019320159852241)
XLA Ops:
  0.6 95.3 %window_attention.1 = (bf16[4,64,3072]{2,1,0:T(8,128)(2,1)}, bf16[2,64,3072]{2,1,0:T(8,128)(2,1)}) custom-call(bf16[64,3072]{1,0:T(8,128)(2,1)} %q_ref.1, bf16[64,3072]{1,0:T(8,128)(2,1)} %k_ref.1, bf16[64,3072]{1,0:T(8,128)(2,1)} %v_ref.1, bf16[64,3072]{1,0:T(8,128)(2,1)} %g_ref.1, s32[8,27]{1,0:T(8,128)} %list_ref.1, s32[256]{0:T(256)} %count_ref.1), custom_call_target="tpu_custom_call" | custom-call | flops 5400000000 | bytes 6000000 | tf_op jit(solution)/shard_map/window_attention/pallas_call | solution.py:600
  95.9 2.3 %relay.1 = (bf16[64,3072]{1,0:T(8,128)(2,1)}, bf16[64,3072]{1,0:T(8,128)(2,1)}, bf16[64,3072]{1,0:T(8,128)(2,1)}, bf16[64,3072]{1,0:T(8,128)(2,1)}) custom-call(bf16[4,64,3072]{2,1,0:T(8,128)(2,1)} %get-tuple-element.6.tokens, bf16[2,64,3072]{2,1,0:T(8,128)(2,1)} %get-tuple-element.7.extra), custom_call_target="tpu_custom_call" | custom-call | tf_op jit(solution)/shard_map/relay/pallas_call | solution.py:632

commit v9 on v8

--- a/solution.py
+++ b/solution.py
@@ -482,12 +482,13 @@
 
             def one(layer, carry):
                 strip(layer, r)
-                send_strip(layer, r)
                 send_edge(i, layer)
 
                 @pl.when(i == 3)
                 def _():
                     send_edge(4, layer)
+
+                send_strip(layer, r)
 
                 @pl.when(jnp.logical_and(i > 0, layer == 0))
                 def _():

time: 98.5 us -> 98.5 us (level)
  no operation moved by 1% of the time
where the time goes in v9:
time: 98.5 us; the launch traced here: 98.4 us
  Pallas kernels  97.7 us (99%)
    pallas_call x1, Pallas kernels, on_device(): pl.pallas_call(kernel, out_shape=(jax.ShapeDtypeStruct((4, TILE, D), BF16...  95.4 us
    pallas_call x1, Pallas kernels, on_device(): pl.pallas_call(relay_kernel, out_shape=(jax.ShapeDtypeStruct((TILE, D), B...  2.33 us

profile of v9, /device:TPU:1, one launch (start us, length us, event | category | flops | bytes accessed | tf_op | source)
XLA Modules:
  0.0 98.4 jit_solution(15871486182026638937)
XLA Ops:
  0.6 95.4 %window_attention.1 = (bf16[4,64,3072]{2,1,0:T(8,128)(2,1)}, bf16[2,64,3072]{2,1,0:T(8,128)(2,1)}) custom-call(bf16[64,3072]{1,0:T(8,128)(2,1)} %q_ref.1, bf16[64,3072]{1,0:T(8,128)(2,1)} %k_ref.1, bf16[64,3072]{1,0:T(8,128)(2,1)} %v_ref.1, bf16[64,3072]{1,0:T(8,128)(2,1)} %g_ref.1, s32[8,27]{1,0:T(8,128)} %list_ref.1, s32[256]{0:T(256)} %count_ref.1), custom_call_target="tpu_custom_call" | custom-call | flops 5400000000 | bytes 6000000 | tf_op jit(solution)/shard_map/window_attention/pallas_call | solution.py:601
  96.0 2.3 %relay.1 = (bf16[64,3072]{1,0:T(8,128)(2,1)}, bf16[64,3072]{1,0:T(8,128)(2,1)}, bf16[64,3072]{1,0:T(8,128)(2,1)}, bf16[64,3072]{1,0:T(8,128)(2,1)}) custom-call(bf16[4,64,3072]{2,1,0:T(8,128)(2,1)} %get-tuple-element.6.tokens, bf16[2,64,3072]{2,1,0:T(8,128)(2,1)} %get-tuple-element.7.extra), custom_call_target="tpu_custom_call" | custom-call | tf_op jit(solution)/shard_map/relay/pallas_call | solution.py:633

commit v10 on v9

--- a/solution.py
+++ b/solution.py
@@ -216,13 +216,7 @@
     def forward(i, carry):
         row = row_of(i)
         for side in range(2):
-            @pl.when(i > 0)
-            def _():
-                wait_for(pool.at[1 + side, row], kv_sem.at[side, jnp.maximum(row, 1) - 1])
-
-            @pl.when(i == 0)
-            def _():
-                wait_for(pool.at[1 + side, row], zsem.at[side])
+            wait_for(pool.at[1 + side, row], kv_sem.at[side, row - 1])
 
             @pl.when(jnp.logical_and(i == 1, other_z // 4 != side))
             def _():
@@ -241,15 +235,27 @@
 
         return carry
 
+    def forward_border(side):
+        row = row_of(0)
+        wait_for(pool.at[1 + side, row], zsem.at[side])
+
+        @pl.when(jnp.where(side == 0, x, NX - 1 - x) > 0)
+        def _():
+            send(
+                pool.at[1 + side, row], pool.at[3 - 3 * side, row], xsend.at[side], xsem.at[1 - side, row],
+                jnp.where(side == 0, low_seat, high_seat), m,
+            )
+
     def forward_own(number):
         @pl.when(jnp.logical_and(active, wave == number))
         def _():
             lax.fori_loop(1, 5, forward, 0)
+            forward_border(z // 4)
 
     def forward_other(number):
         @pl.when(jnp.logical_and(active, wave == number))
         def _():
-            forward(0, 0)
+            forward_border(1 - z // 4)
 
     send_flags(0)
     send_kv(0, 0, 8)

time: 98.5 us -> 98.4 us (level)
  no operation moved by 1% of the time
where the time goes in v10:
time: 98.4 us; the launch traced here: 98.3 us
  Pallas kernels  97.6 us (99%)
    pallas_call x1, Pallas kernels, on_device(): pl.pallas_call(kernel, out_shape=(jax.ShapeDtypeStruct((4, TILE, D), BF16...  95.3 us
    pallas_call x1, Pallas kernels, on_device(): pl.pallas_call(relay_kernel, out_shape=(jax.ShapeDtypeStruct((TILE, D), B...  2.33 us

profile of v10, /device:TPU:1, one launch (start us, length us, event | category | flops | bytes accessed | tf_op | source)
XLA Modules:
  0.0 98.3 jit_solution(16683207873362530680)
XLA Ops:
  0.6 95.3 %window_attention.1 = (bf16[4,64,3072]{2,1,0:T(8,128)(2,1)}, bf16[2,64,3072]{2,1,0:T(8,128)(2,1)}) custom-call(bf16[64,3072]{1,0:T(8,128)(2,1)} %q_ref.1, bf16[64,3072]{1,0:T(8,128)(2,1)} %k_ref.1, bf16[64,3072]{1,0:T(8,128)(2,1)} %v_ref.1, bf16[64,3072]{1,0:T(8,128)(2,1)} %g_ref.1, s32[8,27]{1,0:T(8,128)} %list_ref.1, s32[256]{0:T(256)} %count_ref.1), custom_call_target="tpu_custom_call" | custom-call | flops 5400000000 | bytes 6000000 | tf_op jit(solution)/shard_map/window_attention/pallas_call | solution.py:607
  96.0 2.3 %relay.1 = (bf16[64,3072]{1,0:T(8,128)(2,1)}, bf16[64,3072]{1,0:T(8,128)(2,1)}, bf16[64,3072]{1,0:T(8,128)(2,1)}, bf16[64,3072]{1,0:T(8,128)(2,1)}) custom-call(bf16[4,64,3072]{2,1,0:T(8,128)(2,1)} %get-tuple-element.6.tokens, bf16[2,64,3072]{2,1,0:T(8,128)(2,1)} %get-tuple-element.7.extra), custom_call_target="tpu_custom_call" | custom-call | tf_op jit(solution)/shard_map/relay/pallas_call | solution.py:639
